TPU v7x, 32 devices: a whole 2x2x4 slice. The times are simulated.
32 devices in a mesh: dp: 16 (over z, x, core), state: 2 (over y).
Axes of the slice: x: 2, y: 2, z: 4, core: 2. Of those that a mesh axis runs over, the one named last changes fastest.
Arguments:
- tokens: bfloat16 [2, 2048, 1024], P(None, 'dp'), may hold values from -6 to 6
- cluster_len: int32 [2, 16, 2], P(None, 'dp'), may hold values from 32 to 96, as said below
- norm_gain: float32 [1024], replicated, may hold values from 0.1 to 1.9
- in_weight: bfloat16 [4096, 1024], replicated, may hold values from -0.1875 to 0.1875
- conv_weight: float32 [4, 2048], replicated, may hold values from -3 to 3
- conv_bias: float32 [2048], replicated, may hold values from -1.5 to 1.5
- dtx_weight: bfloat16 [2048, 64], replicated, may hold values from -0.125 to 0.125
- dt_weight: bfloat16 [2048, 64], replicated, may hold values from -0.75 to 0.75
- dt_bias: float32 [2048], replicated, may hold values from -7 to -2.3
- bc_weight: bfloat16 [2, 16, 2048], P(None, 'state'), may hold values from -0.125 to 0.125
- a_log: float32 [16, 2048], P('state'), may hold values from -1 to 2.8
- skip_gain: float32 [2048], replicated, may hold values from 0.1 to 1.9
- out_weight: bfloat16 [2048, 1024], replicated, may hold values from -0.125 to 0.125
- cotangent: bfloat16 [2, 2048, 1024], P(None, 'dp'), may hold values from -6 to 6
Outputs:
- mixed: bfloat16 [2, 2048, 1024], P(None, 'dp')
- tokens_grad: float32 [2, 2048, 1024], P(None, 'dp')
- gain_grad: float32 [1024], P(('dp', 'state'))
- in_grad: float32 [4096, 1024], P(('dp', 'state'))
- conv_weight_grad: float32 [4, 2048], P(None, ('dp', 'state'))
- conv_bias_grad: float32 [2048], P(('dp', 'state'))
- dtx_grad: float32 [2048, 64], P(('dp', 'state'))
- dt_weight_grad: float32 [2048, 64], P(('dp', 'state'))
- dt_bias_grad: float32 [2048], P(('dp', 'state'))
- bc_grad: float32 [2, 16, 2048], P(None, 'state', 'dp')
- a_log_grad: float32 [16, 2048], P('state', 'dp')
- skip_grad: float32 [2048], P(('dp', 'state'))
- out_grad: float32 [2048, 1024], P(('dp', 'state'))
Inputs may be any that keep to these rules, and one draw needn't show every extreme that they name: `cluster_len`: in each row the 2 lengths sum to 128; one of them equals 96, the other 32.
All inputs are finite; a program needn't handle non-finite values.
Results may differ from a plain program's by a relative error of at most 0.012.
Values may be sent and summed in bfloat16 or wider, within the bound.
No kernel may reach another device: no remote copies, remote signals or barrier semaphores. Data moves between devices by JAX's collectives and lax.ppermute only.
A program may use at most 256 MiB of HBM per device.

v0:
```python
import functools
import math

import jax
import jax.numpy as jnp
from jax import lax
from jax.experimental import pallas as pl
from jax.experimental.pallas import tpu as pltpu
from jax.sharding import PartitionSpec as P

EPSILON = 1e-05
LANES = 128
RESET = 1e4
LOG2E = math.log2(math.e)
F32 = jnp.float32
BF16 = jnp.bfloat16
MIB = 1024 * 1024


def dot(left, right, left_dim, right_dim):
    return lax.dot_general(
        left, right, (((left_dim,), (right_dim,)), ((), ())), preferred_element_type=F32
    )


def params(mib):
    return pltpu.CompilerParams(
        vmem_limit_bytes=mib * MIB, dimension_semantics=("arbitrary",)
    )


ANY = pl.BlockSpec(memory_space=pl.ANY)


def stream(step, steps, fetch):
    @pl.when(step == 0)
    def _():
        for k in range(steps):
            for copy in fetch(k):
                copy.start()

    for copy in fetch(step):
        copy.wait()


def whole(shape):
    return pl.BlockSpec(shape, lambda *_: (0,) * len(shape))


sigmoid = jax.nn.sigmoid


def log_one_plus(value):
    series = value * (1.0 - value * (0.5 - value * (1.0 / 3.0)))
    return jnp.where(value < 1e-3, series, jnp.log(1.0 + value))


def lanes(index):
    return pl.ds(pl.multiple_of(index * LANES, LANES), LANES)


def cost(micros):
    return pl.CostEstimate(
        flops=int(micros * 1e9), bytes_accessed=int(micros * 1e6), transcendentals=0
    )


def hbm(shape, dtype):
    return pltpu.HBM(shape, dtype)


def in_hbm(arrays):
    return [pltpu.with_memory_space_constraint(array, pltpu.HBM) for array in arrays]


def aligned(start, size, to=8):
    return pl.ds(pl.multiple_of(start, to), size)


SEGMENTS = 4

HALF, CORE, CUBE, FACE = range(4)


def fill_masks(len_ref, mask_ref, micros, count, taps, clusters):
    place = lax.broadcasted_iota(jnp.int32, (count, LANES), 0)
    for micro in range(micros):
        rows = pl.ds(micro * count, count)
        for back in range(1, taps):
            apart = place < back
            start = 0
            for cluster in range(clusters - 1):
                start = start + len_ref[micro, 0, cluster]
                apart = apart | ((place >= start) & (place < start + back))
            mask_ref[back, rows, :] = jnp.where(apart, 0.0, 1.0)
            if back == 1:
                mask_ref[0, rows, :] = jnp.where(apart, 1.0, 0.0)


def project_kernel(
    place_ref,
    len_ref,
    gain_ref,
    convw_ref,
    convb_ref,
    x_far,
    weight_far,
    normed_far,
    act_far,
    own_act_far,
    inner_far,
    bend_far,
    gate_far,
    mask_ref,
    x_ref,
    win_ref,
    wgate_ref,
    normed_ref,
    act_ref,
    own_act_ref,
    inner_ref,
    bend_ref,
    gate_ref,
    in_sems,
    out_sems,
    *,
    micros,
    count,
    taps,
    clusters,
):
    half = place_ref[HALF]
    chunks = win_ref.shape[0]
    inward = [pltpu.make_async_copy(x_far, x_ref, in_sems.at[2 * chunks])]
    for k in range(chunks):
        inward.append(pltpu.make_async_copy(weight_far.at[0, k], win_ref.at[k], in_sems.at[2 * k]))
        inward.append(
            pltpu.make_async_copy(
                weight_far.at[1, k, half], wgate_ref.at[k], in_sems.at[2 * k + 1]
            )
        )
    for copy in inward:
        copy.start()
    outward = []

    def put(source, target):
        outward.append(pltpu.make_async_copy(source, target, out_sems.at[len(outward)]))
        outward[-1].start()

    fill_masks(len_ref, mask_ref, micros, count, taps, clusters)
    inward[0].wait()
    rows = x_ref[...].astype(F32)
    scale = lax.rsqrt(jnp.mean(rows * rows, axis=1, keepdims=True) + EPSILON)
    normed = (rows * scale * gain_ref[...]).astype(BF16)
    normed_ref[...] = normed
    put(normed_ref, normed_far)
    for k in range(chunks):
        inward[2 * k + 1].wait()
        inward[2 * k + 2].wait()
        proj = dot(normed, win_ref[k].reshape(2 * LANES, -1), 1, 1)
        own = slice(k * LANES, (k + 1) * LANES)
        gate_ref[:, own] = dot(normed, wgate_ref[k], 1, 1)
        inners, sigs, acts = [], [], []
        for part in range(2):
            cols = slice((2 * k + part) * LANES, (2 * k + part + 1) * LANES)
            inner = proj[:, part * LANES : (part + 1) * LANES]
            conved = convb_ref[2 * k + part : 2 * k + part + 1, :]
            conved = conved + convw_ref[taps - 1 : taps, cols] * inner
            for back in range(1, taps):
                shifted = pltpu.roll(inner, back, 0) * mask_ref[back]
                conved = conved + convw_ref[taps - 1 - back : taps - back, cols] * shifted
            sig = sigmoid(conved)
            act = conved * sig
            act_ref[:, cols] = act.astype(BF16)
            inners.append(inner)
            sigs.append(sig)
            acts.append(act)
        inner_ref[:, own] = jnp.where(half == 0, *inners)
        act, sig = jnp.where(half == 0, *acts), jnp.where(half == 0, *sigs)
        bend_ref[:, own] = (sig + act * (1.0 - sig)).astype(BF16)
        own_act_ref[:, own] = act.astype(BF16)
        if k % 2:
            group = pl.ds((k - 1) * LANES, 2 * LANES)
            wide = pl.ds(2 * (k - 1) * LANES, 4 * LANES)
            put(act_ref.at[:, wide], act_far.at[:, wide])
            for near, far in (
                (gate_ref, gate_far),
                (inner_ref, inner_far),
                (bend_ref, bend_far),
                (own_act_ref, own_act_far),
            ):
                put(near.at[:, group], far.at[:, group])
    for copy in outward:
        copy.wait()


def project(place, lengths, x, gain, w4, conv_weight, conv_bias):
    rows, width = x.shape
    chunks = w4.shape[1]
    micros, _, clusters = lengths.shape
    taps = conv_weight.shape[0]
    own = chunks * LANES
    outs = [
        ((rows, width), BF16),
        ((rows, 2 * own), BF16),
        ((rows, own), BF16),
        ((rows, own), F32),
        ((rows, own), BF16),
        ((rows, own), F32),
    ]
    return pl.pallas_call(
        functools.partial(
            project_kernel, micros=micros, count=rows // micros, taps=taps, clusters=clusters
        ),
        grid_spec=pltpu.PrefetchScalarGridSpec(
            num_scalar_prefetch=1,
            grid=(1,),
            in_specs=[
                pl.BlockSpec(memory_space=pltpu.SMEM),
                whole(gain.shape),
                whole(conv_weight.shape),
                whole(conv_bias.shape),
                ANY,
                ANY,
            ],
            out_specs=[ANY] * len(outs),
            scratch_shapes=[
                pltpu.VMEM((taps, rows, LANES), F32),
                pltpu.VMEM((rows, width), BF16),
                pltpu.VMEM((chunks, 2, LANES, width), BF16),
                pltpu.VMEM((chunks, LANES, width), BF16),
            ]
            + [pltpu.VMEM(*out) for out in outs]
            + [
                pltpu.SemaphoreType.DMA((2 * chunks + 1,)),
                pltpu.SemaphoreType.DMA((1 + 5 * chunks // 2,)),
            ],
        ),
        out_shape=[hbm(*out) for out in outs],
        compiler_params=params(30),
        cost_estimate=cost(6),
        name="project",
    )(place, *in_hbm((lengths, gain, conv_weight, conv_bias, x, w4)))


def every_row(ref, row, height):
    return ref[pl.ds(row, height, stride=0), :]


def b_at(n, eighth):
    return (n // eighth) * 2 * eighth + n % eighth


def c_at(n, eighth):
    return b_at(n, eighth) + eighth


def forward_kernel(
    place_ref,
    len_ref,
    act_all_ref,
    bc_own_ref,
    bc_other_ref,
    alog_own_ref,
    alog_other_ref,
    dtx_ref,
    dt_ref,
    bias_ref,
    skip_ref,
    act_ref,
    *refs,
    micros,
    count,
    states,
    chunks,
    clusters,
):
    gate_far, wout_far, cotan_far, normed_far = refs[:4]
    bc_ref, rank_ref, rank_high_ref, decay_ref = refs[4:8]
    sp_far, u_far, step_far, slope_far, h_far, dy_far = refs[8:14]
    gated_far, dgate_far, keep_far, send_far = refs[14:18]
    mask_ref, y_ref, tmp_ref, wide_ref = refs[18:22]
    gate_ref, wout_ref, cotan_ref, normed_ref = refs[22:26]
    sp_ref, u_ref, step_ref, slope_ref, h_ref, dy_ref = refs[26:32]
    gated_ref, dgate_ref, keep_ref, send_ref = refs[32:36]
    in_sems, out_sems = refs[36:]
    rows = micros * count
    eighth = states // 2
    half, core, cube, face = (place_ref[k] for k in range(4))
    first = half == 0
    inward = [
        pltpu.make_async_copy(source, target, in_sems.at[k])
        for k, (source, target) in enumerate(
            (
                (gate_far, gate_ref),
                (wout_far.at[:, half], wout_ref),
                (cotan_far, cotan_ref),
                (normed_far, normed_ref),
            )
        )
    ]
    for copy in inward:
        copy.start()
    outward = []

    def put(source, target):
        outward.append(pltpu.make_async_copy(source, target, out_sems.at[len(outward)]))
        outward[-1].start()

    ranks = dtx_ref.shape[0]
    weights = jnp.concatenate(
        [dtx_ref[...]] + [ref[...].reshape(states, -1) for ref in (bc_own_ref, bc_other_ref)]
    )
    product = dot(act_all_ref[...], weights, 1, 1)
    own, other = product[:, ranks : ranks + states], product[:, ranks + states :]
    bc_ref[:, :states] = jnp.where(first, own, other)
    bc_ref[:, states:] = jnp.where(first, other, own)
    spread_lanes(bc_ref, wide_ref)

    fill_masks(len_ref, mask_ref, micros, count, 2, clusters)
    for chunk in range(chunks):
        cols = lanes(2 * chunk + half)
        own, other = alog_own_ref[:, cols], alog_other_ref[:, cols]
        tmp_ref[pl.ds(chunk * states, eighth), :] = jnp.where(first, own, other)
        tmp_ref[pl.ds(chunk * states + eighth, eighth), :] = jnp.where(first, other, own)
    for n in range(states):
        decay_ref[pl.ds(n * chunks, chunks), :] = -LOG2E * jnp.exp(
            tmp_ref[pl.ds(n, chunks, stride=states), :]
        )

    rank = product[:, :ranks].astype(BF16)
    rank_ref[...] = rank
    rank_high_ref[...] = jnp.concatenate([jnp.zeros_like(rank), rank], axis=1)
    for chunk in range(chunks):
        cols = slice(chunk * LANES, (chunk + 1) * LANES)
        bias = bias_ref[pl.ds(2 * chunk + half, 1), :]
        pre = dot(rank, dt_ref[:, lanes(2 * chunk + half)], 1, 0) + bias
        tail_part = jnp.exp(-jnp.abs(pre))
        step = jnp.maximum(pre, 0.0) + log_one_plus(tail_part)
        slope = jnp.where(pre >= 0.0, 1.0, tail_part) / (1.0 + tail_part)
        step_ref[:, cols] = step
        slope_ref[:, cols] = slope.astype(BF16)
        held = step + RESET * mask_ref[0]
        source = step * act_ref[:, cols].astype(F32)
        for micro in range(micros):
            span = slice(micro * count, (micro + 1) * count)
            place = pl.ds((micro * chunks + chunk) * count, count)
            sp_ref[place, :] = held[span]
            u_ref[place, :] = source[span]
    put(sp_ref, sp_far)
    put(u_ref, u_far)
    put(step_ref, step_far)
    put(slope_ref, slope_far)

    for micro in range(micros):

        def advance(t, h, micro=micro):
            row = micro * count + t
            span = pl.ds(micro * chunks * count + t, chunks, stride=count)
            sp = sp_ref[span, :]
            u = u_ref[span, :]
            out = []
            y = None
            for n in range(states):
                decay = jnp.exp2(sp * decay_ref[pl.ds(n * chunks, chunks), :])
                now = decay * h[n] + u * every_row(wide_ref, b_at(n, eighth) * rows + row, chunks)
                h_ref[aligned((row * states + n) * chunks, chunks), :] = now
                out.append(now)
                term = now * every_row(wide_ref, c_at(n, eighth) * rows + row, chunks)
                y = term if y is None else y + term
            y_ref[span, :] = y
            return tuple(out)

        h = (jnp.zeros((chunks, LANES), F32),) * states
        segment = count // SEGMENTS
        for k in range(SEGMENTS):
            h = lax.fori_loop(k * segment, (k + 1) * segment, advance, h, unroll=8)
            extent = segment * states * chunks
            place = pl.ds((micro * SEGMENTS + k) * extent, extent)
            put(h_ref.at[place], h_far.at[place])

    for copy in inward:
        copy.wait()
    cotan = cotan_ref[...]
    for chunk in range(chunks):
        cols = slice(chunk * LANES, (chunk + 1) * LANES)
        places = [pl.ds((micro * chunks + chunk) * count, count) for micro in range(micros)]
        y = jnp.concatenate([y_ref[place, :] for place in places])
        y = y + skip_ref[pl.ds(2 * chunk + half, 1), :] * act_ref[:, cols].astype(F32)
        gate = gate_ref[:, cols]
        sig = sigmoid(gate)
        gated_ref[:, cols] = (y * (gate * sig)).astype(BF16)
        dgated = dot(cotan, wout_ref[chunk], 1, 1)
        dy = dgated * (gate * sig)
        for micro in range(micros):
            dy_ref[places[micro], :] = dy[micro * count : (micro + 1) * count]
        dgate_ref[:, cols] = (dgated * y * (sig * (1.0 + gate * (1.0 - sig)))).astype(BF16)
    put(dy_ref, dy_far)
    put(gated_ref, gated_far)
    put(dgate_ref, dgate_far)
    normed = normed_ref[...]
    edge = LANES // 2
    for r in range(chunks // 2):
        for zh in range(2):
            grad = dot(gated_ref[:, lanes((r + 4 * zh) ^ cube)], cotan, 0, 0).astype(BF16)
            top, bottom = grad[:edge], grad[edge:]
            place = pl.ds(r * 2 * LANES + zh * edge, edge)
            keep_ref[place, :] = jnp.where(core == 0, top, bottom)
            send_ref[place, :] = jnp.where(core == 0, bottom, top)
        place = pl.ds((2 * r + 1) * LANES, LANES)
        pair = 2 * (r ^ face)
        for chunk, out_ref in ((pair + core, keep_ref), (pair + 1 - core, send_ref)):
            out_ref[place, :] = dot(dgate_ref[:, lanes(chunk)], normed, 0, 0).astype(BF16)
        place = pl.ds(r * 2 * LANES, 2 * LANES)
        put(send_ref.at[place], send_far.at[place])
        put(keep_ref.at[place], keep_far.at[place])
    for copy in outward:
        copy.wait()


def scan_forward(
    place,
    lengths,
    act_all,
    bc_own,
    bc_other,
    alog_own,
    alog_other,
    dtx,
    dt,
    bias,
    skip,
    act,
    gate,
    wout3,
    cotan,
    normed,
):
    rows, own = act.shape
    chunks = own // LANES
    states = 2 * alog_own.shape[0]
    width = cotan.shape[1]
    micros, _, clusters = lengths.shape
    ranks = dtx.shape[0]
    small = [
        ((rows, 2 * states), F32),
        ((rows, ranks), BF16),
        ((rows, 2 * ranks), BF16),
        ((states * chunks, LANES), F32),
    ]
    large = [
        ((chunks * rows, LANES), F32),
        ((chunks * rows, LANES), F32),
        ((rows, own), F32),
        ((rows, own), BF16),
        ((rows * states * chunks, LANES), F32),
        ((chunks * rows, LANES), F32),
        ((rows, own), BF16),
        ((rows, own), BF16),
        ((own, width), BF16),
        ((own, width), BF16),
    ]
    operands = (act_all, bc_own, bc_other, alog_own, alog_other, dtx, dt, bias, skip, act)
    streamed = (gate, wout3, cotan, normed)
    return pl.pallas_call(
        functools.partial(
            forward_kernel,
            micros=micros,
            count=rows // micros,
            states=states,
            chunks=chunks,
            clusters=clusters,
        ),
        grid_spec=pltpu.PrefetchScalarGridSpec(
            num_scalar_prefetch=1,
            grid=(1,),
            in_specs=[pl.BlockSpec(memory_space=pltpu.SMEM)]
            + [whole(operand.shape) for operand in operands]
            + [ANY] * len(streamed),
            out_specs=[whole(shape) for shape, _ in small] + [ANY] * len(large),
            scratch_shapes=[
                pltpu.VMEM((2, rows, LANES), F32),
                pltpu.VMEM((chunks * rows, LANES), F32),
                pltpu.VMEM((states * chunks, LANES), F32),
                pltpu.VMEM((2 * states * rows + 8, LANES), F32),
                pltpu.VMEM((rows, own), F32),
                pltpu.VMEM((chunks, LANES, width), BF16),
                pltpu.VMEM((rows, width), BF16),
                pltpu.VMEM((rows, width), BF16),
            ]
            + [pltpu.VMEM(*out) for out in large]
            + [pltpu.SemaphoreType.DMA((4,)), pltpu.SemaphoreType.DMA((7 + chunks + micros * SEGMENTS,))],
        ),
        out_shape=[hbm(*out) for out in small + large],
        compiler_params=params(52),
        cost_estimate=cost(19),
        name="scan_forward",
    )(
        place,
        lengths,
        *in_hbm(operands[:1]),
        *operands[1:5],
        *in_hbm((*operands[5:], *streamed)),
    )


def spread_lanes(values_ref, wide_ref):
    rows, count = values_ref.shape
    for k in range(count):
        wide_ref[pl.ds(k * rows, rows), :] = jnp.broadcast_to(
            values_ref[:, k : k + 1], (rows, LANES)
        )


def backward_kernel(
    place_ref,
    bc_ref,
    decay_ref,
    dt_ref,
    skip_ref,
    act_ref,
    sp_ref,
    u_ref,
    step_ref,
    slope_ref,
    dy_ref,
    h_far,
    code_ref,
    sact_ref,
    dpre_ref,
    alog_ref,
    vec_ref,
    h_ref,
    s_ref,
    d_ref,
    terms_ref,
    sums_b_ref,
    sums_c_ref,
    wide_ref,
    sems,
    *,
    count,
    states,
    chunks,
):
    micro = pl.program_id(0)
    block = states * chunks
    segment = count // SEGMENTS

    def fetch(which, k):
        extent = segment * block
        buffer = h_ref.at[which % 2]
        return pltpu.make_async_copy(
            h_far.at[aligned((which * SEGMENTS + k) * extent, extent)],
            buffer.at[pl.ds(block + k * extent, extent)],
            sems.at[which % 2, k],
        )

    @pl.when(micro == 0)
    def _():
        for k in reversed(range(SEGMENTS)):
            fetch(0, k).start()
        for which in range(2):
            h_ref[which, pl.ds(0, block), :] = jnp.zeros((block, LANES), F32)
        alog_ref[...] = jnp.zeros_like(alog_ref)
        vec_ref[...] = jnp.zeros_like(vec_ref)

    half = place_ref[HALF]
    eighth = states // 2
    zero = (jnp.zeros((chunks, LANES), F32),) * states
    spread_lanes(bc_ref, wide_ref)

    @pl.when(micro + 1 < pl.num_programs(0))
    def _():
        for k in reversed(range(SEGMENTS)):
            fetch(micro + 1, k).start()

    side = micro % 2

    def put_terms(which, t, terms):
        for n in range(0, states, 2):
            pair = jnp.concatenate(terms[n : n + 2]).astype(BF16)
            place = aligned(t * block + n * chunks, 2 * chunks, 16)
            terms_ref[which, place, :] = pair

    def retreat(back, carry):
        flows, totals = carry
        for slot in range(4):
            t = count - 1 - (4 * back + slot)
            span = pl.ds(t, chunks, stride=count)
            sp = sp_ref[span, :]
            u = u_ref[span, :]
            dy = dy_ref[span, :]
            out_flows = []
            out_totals = []
            b_terms, c_terms = [], []
            d_sum = None
            s_sum = None
            for n in range(states):
                rate = decay_ref[pl.ds(n * chunks, chunks), :]
                dh = flows[n] + dy * every_row(wide_ref, c_at(n, eighth) * count + t, chunks)
                flow = jnp.exp2(sp * rate) * dh
                out_flows.append(flow)
                q = flow * h_ref[side, aligned(t * block + n * chunks, chunks), :]
                now = h_ref[side, aligned((t + 1) * block + n * chunks, chunks), :]
                out_totals.append(totals[n] + q * sp)
                d_term = q * rate
                s_term = dh * every_row(wide_ref, b_at(n, eighth) * count + t, chunks)
                d_sum = d_term if d_sum is None else d_sum + d_term
                s_sum = s_term if s_sum is None else s_sum + s_term
                b_terms.append(dh * u)
                c_terms.append(dy * now)
            s_ref[span, :] = s_sum
            d_ref[span, :] = d_sum
            put_terms(0, t, b_terms)
            put_terms(1, t, c_terms)
            flows, totals = tuple(out_flows), tuple(out_totals)
        return flows, totals

    carry = (zero, zero)
    for k in range(SEGMENTS):
        fetch(micro, SEGMENTS - 1 - k).wait()
        carry = lax.fori_loop(k * segment // 4, (k + 1) * segment // 4, retreat, carry)
    totals = carry[1]
    for n in range(states):
        alog_ref[pl.ds(n * chunks, chunks), :] += totals[n]

    shape = (2 * states, 2 * block)
    group = lax.broadcasted_iota(jnp.int32, shape, 1) // chunks
    gather = jnp.where(group == lax.broadcasted_iota(jnp.int32, shape, 0), 1.0, 0.0).astype(BF16)

    @pl.loop(0, count // 64)
    def _(step):
        for which, sums_ref in ((0, sums_b_ref), (1, sums_c_ref)):
            for k in range(32):
                at = 32 * step + k
                terms = terms_ref[which, aligned(at * 2 * block, 2 * block, 16), :]
                sums_ref[aligned(at * 2 * states, 2 * states), :] = dot(gather, terms, 1, 0)

    ranks = dt_ref.shape[0]
    drank = None
    for chunk in range(chunks):
        cols = slice(chunk * LANES, (chunk + 1) * LANES)
        place = pl.ds(chunk * count, count)
        act = act_ref[:, cols].astype(F32)
        weight = dt_ref[:, lanes(2 * chunk + half)]
        s_now = s_ref[place, :]
        dstep = d_ref[place, :] * (1.0 / LOG2E) + s_now * act
        dy = dy_ref[place, :]
        skip = skip_ref[pl.ds(2 * chunk + half, 1), :]
        sact_ref[:, cols] = s_now * step_ref[:, cols] + dy * skip
        dpre = dstep * slope_ref[:, cols].astype(F32)
        vec_ref[0:1, cols] += jnp.sum(dpre, axis=0, keepdims=True)
        vec_ref[1:2, cols] += jnp.sum(dy * act, axis=0, keepdims=True)
        low = dpre.astype(BF16)
        dpre_ref[:, cols] = low
        term = dot(low, weight, 1, 1)
        drank = term if drank is None else drank + term
    source = lax.broadcasted_iota(jnp.int32, (2 * LANES, LANES), 0)
    target = lax.broadcasted_iota(jnp.int32, (2 * LANES, LANES), 1)
    code = None
    for n in range(states):
        pair = jnp.concatenate(
            [ref[pl.ds(n, count, stride=states), :] for ref in (sums_b_ref, sums_c_ref)], axis=1
        )
        column = ranks + jnp.where(source < LANES, b_at(n, eighth), c_at(n, eighth))
        pick = jnp.where(target == column, 1.0, 0.0).astype(BF16)
        term = dot(pair.astype(BF16), pick, 1, 0)
        code = term if code is None else code + term
    drank = jnp.concatenate([drank, jnp.zeros((count, LANES - ranks), F32)], axis=1)
    code_ref[...] = (code + drank).astype(BF16)


def scan_backward(place, micros, bc, decay, dt, skip, act, sp, u, step, slope, dy, h):
    rows, own = act.shape
    count = rows // micros
    chunks = own // LANES
    states = bc.shape[1] // 2
    outs = [
        ((rows, LANES), BF16),
        ((rows, own), F32),
        ((rows, own), BF16),
        ((states * chunks, LANES), F32),
        ((2, own), F32),
    ]

    def block(*shape):
        return pl.BlockSpec(shape, lambda i, p: (i, 0))

    return pl.pallas_call(
        functools.partial(backward_kernel, count=count, states=states, chunks=chunks),
        grid_spec=pltpu.PrefetchScalarGridSpec(
            num_scalar_prefetch=1,
            grid=(micros,),
            in_specs=[
                block(count, 2 * states),
                whole(decay.shape),
                whole(dt.shape),
                whole(skip.shape),
                block(count, own),
                block(chunks * count, LANES),
                block(chunks * count, LANES),
                block(count, own),
                block(count, own),
                block(chunks * count, LANES),
                ANY,
            ],
            out_specs=[block(count, LANES), block(count, own), block(count, own)]
            + [whole(shape) for shape, _ in outs[3:]],
            scratch_shapes=[
                pltpu.VMEM((2, (count + 1) * states * chunks, LANES), F32),
                pltpu.VMEM((chunks * count, LANES), F32),
                pltpu.VMEM((chunks * count, LANES), F32),
                pltpu.VMEM((2, count * states * chunks, LANES), BF16),
                pltpu.VMEM((count * states, LANES), F32),
                pltpu.VMEM((count * states, LANES), F32),
                pltpu.VMEM((2 * states * count + 8, LANES), F32),
                pltpu.SemaphoreType.DMA((2, SEGMENTS)),
            ],
        ),
        out_shape=[hbm(*out) for out in outs],
        compiler_params=params(52),
        cost_estimate=cost(0),
        name="scan_backward",
    )(place, *in_hbm((bc, decay, dt, skip, act, sp, u, step, slope, dy, h)))


def tail_kernel(
    place_ref,
    len_ref,
    *refs,
    micros,
    count,
    taps,
    clusters,
    ranks,
    chunks,
    states,
):
    def take(number):
        nonlocal refs
        taken, refs = refs[:number], refs[number:]
        return taken

    code_own_ref, code_other_ref = take(2)
    sact_ref, dpre_ref, alog_sum_ref, back_ref = take(4)
    dtx_ref, bc_own_ref, bc_other_ref, decay_ref = take(4)
    bend_ref, inner_ref, act_ref, high_ref, convw_ref = take(5)
    normed_ref, weight_ref, gate_part_ref, x_ref = take(4)
    keep_ref, send_ref, dnormed_ref = take(3)
    mask_ref, code_ref, wcode_ref, vec_ref, alog_ref, total_ref, win_ref, sems, low_ref = refs[:9]
    code_turned_ref, rank_turned_ref = refs[9:]

    step = pl.program_id(0)
    rows = micros * count
    eighth = states // 2
    edge = LANES // 2
    half, core, cube, face = (place_ref[k] for k in range(4))
    pair = step ^ face
    span = LANES + 32

    def fetch(k):
        source = weight_ref.at[0, pl.ds(2 * (k ^ face), 2), half]
        return (pltpu.make_async_copy(source, win_ref.at[k], sems.at[k]),)

    stream(step, win_ref.shape[0], fetch)

    def pack_row(chunk):
        relative = chunk ^ cube
        return (relative & 3) * span + LANES + (relative >> 2) * 16

    def place_pair(start, size, cols, even, odd):
        keep_ref[aligned(start, size, 16), cols] = jnp.where(core == 0, even, odd).astype(BF16)
        send_ref[aligned(start, size, 16), cols] = jnp.where(core == 0, odd, even).astype(BF16)

    @pl.when(step == 0)
    def _():
        fill_masks(len_ref, mask_ref, micros, count, taps, clusters)
        total_ref[...] = gate_part_ref[...].astype(F32)
        code_ref[...] = (
            code_own_ref[...].astype(F32) + code_other_ref[...].astype(F32)
        ).astype(BF16)
        code_turned_ref[...] = code_ref[...].T
        rank_turned_ref[...] = high_ref[...].T
        alog_ref[...] = alog_sum_ref[...] * (decay_ref[...] * (1.0 / LOG2E))

    code = code_ref[...]
    lane = lax.broadcasted_iota(jnp.int32, (1, LANES), 1)
    for part in range(2):
        source = lanes(2 * (2 * pair + part) + half)
        cols = slice(part * LANES, (part + 1) * LANES)
        wcode_ref[:ranks, cols] = dtx_ref[:, source]
        own = bc_own_ref[:, :, source].reshape(states, LANES)
        other = bc_other_ref[:, :, source].reshape(states, LANES)
        wcode_ref[ranks : ranks + states, cols] = jnp.where(half == 0, own, other)
        wcode_ref[ranks + states : ranks + 2 * states, cols] = jnp.where(half == 0, other, own)
        wcode_ref[ranks + 2 * states :, cols] = jnp.zeros(
            (LANES - ranks - 2 * states, LANES), BF16
        )
    for part in range(2):
        cols = slice(part * LANES, (part + 1) * LANES)
        chunk = 2 * pair + part
        source = 2 * chunk + half
        weights = convw_ref[:, lanes(source)]
        dact = sact_ref[:, cols] + dot(code, wcode_ref[:, cols], 1, 0)
        dconv = dact * bend_ref[:, cols].astype(F32)
        inner = inner_ref[:, cols]
        dinner = weights[taps - 1 : taps] * dconv
        sums = [None] * (taps + 1)
        sums[taps - 1] = jnp.sum(dconv * inner, axis=0, keepdims=True)
        sums[taps] = jnp.sum(dconv, axis=0, keepdims=True)
        for back in range(1, taps):
            kept = dconv * mask_ref[back]
            dinner = dinner + weights[taps - 1 - back : taps - back] * pltpu.roll(
                kept, rows - back, 0
            )
            sums[taps - 1 - back] = jnp.sum(
                kept * pltpu.roll(inner, back, 0), axis=0, keepdims=True
            )
        for k in range(taps + 1):
            vec_ref[k : k + 1, lanes(chunk)] = sums[k]
        vec_ref[taps + 1 : taps + 3, lanes(chunk)] = back_ref[:, lanes(chunk)]
        low_ref[:, cols] = dinner.astype(BF16)

        act = act_ref[:, cols]
        start = pack_row(chunk)
        code_rows = dot(code_turned_ref[...], act, 1, 0)
        rank_rows = dot(rank_turned_ref[...], dpre_ref[:, cols], 1, 0)[ranks:]
        dtx_rows = code_rows[:ranks]
        even = jnp.where(lane < edge, dtx_rows, pltpu.roll(rank_rows, edge, 1))
        odd = jnp.where(lane < edge, pltpu.roll(dtx_rows, edge, 1), rank_rows)
        for k in range(4):
            place = slice(k * 16, (k + 1) * 16)
            place_pair(
                start, 16, slice(k * LANES, (k + 1) * LANES), even[place], odd[place]
            )
        state_rows = code_rows[ranks : ranks + 2 * states]
        place_pair(
            start, 16, slice(4 * LANES, 5 * LANES), state_rows[:states], state_rows[states:]
        )

    normed = normed_ref[...]
    for part in range(2):
        grad = dot(low_ref[:, lanes(core ^ part)], normed, 0, 0)
        out_ref = (keep_ref, send_ref)[part]
        out_ref[aligned(step * span, LANES, 16), :] = grad.astype(BF16)
    width = total_ref.shape[1]
    total_ref[...] += dot(low_ref[...], win_ref[step].reshape(2 * LANES, width), 1, 0)

    @pl.when(step == pl.num_programs(0) - 1)
    def _():
        total = total_ref[...]
        dnormed_ref[...] = total.astype(BF16)
        x = x_ref[...].astype(F32)
        unit = x * lax.rsqrt(jnp.mean(x * x, axis=1, keepdims=True) + EPSILON)
        vec_ref[taps + 3 : taps + 4, :] = jnp.sum(total * unit, axis=0, keepdims=True)
        is_gain = lax.broadcasted_iota(jnp.int32, (8, LANES), 0) == taps + 3
        for chunk in range(chunks):
            start = pack_row(chunk)
            vec = vec_ref[:, chunk * LANES : (chunk + 1) * LANES]
            far, farther = (pltpu.roll(vec, LANES - k * edge // 2, 1) for k in (1, 2))
            even = jnp.where(is_gain & (lane >= edge // 2), far, vec)
            odd = jnp.where(is_gain & (lane < edge // 2), far, farther)
            alog = [
                alog_ref[pl.ds(q * eighth * chunks + chunk, eighth, stride=chunks), :]
                for q in range(2)
            ]
            place_pair(
                start,
                16,
                slice(5 * LANES, 6 * LANES),
                jnp.concatenate([alog[0], even]),
                jnp.concatenate([alog[1], odd]),
            )
            blank = jnp.zeros((16, 2 * LANES), F32)
            place_pair(start, 16, slice(6 * LANES, 8 * LANES), blank, blank)


def tail(
    place,
    lengths,
    code_own,
    code_other,
    sact,
    dpre,
    alog,
    back,
    dtx,
    bc_own,
    bc_other,
    decay,
    bend,
    inner,
    act,
    high,
    convw,
    normed,
    w4,
    gate_part,
    x,
):
    rows, own = act.shape
    chunks = own // LANES
    width = normed.shape[1]
    micros, _, clusters = lengths.shape
    count = rows // micros
    taps = convw.shape[0]
    ranks = dtx.shape[0]
    states = decay.shape[0] // chunks
    cols = 2 * LANES
    extent = 4 * (LANES + 32)

    def by_cols(height):
        return pl.BlockSpec((height, cols), lambda i, p: (0, i ^ p[FACE]))

    in_specs = (
        [pl.BlockSpec(memory_space=pltpu.SMEM)]
        + [whole((rows, LANES))] * 2
        + [by_cols(rows)] * 2
        + [whole(alog.shape), whole(back.shape)]
        + [whole(array.shape) for array in (dtx, bc_own, bc_other, decay)]
        + [by_cols(rows)] * 3
        + [whole(array.shape) for array in (high, convw, normed)]
        + [
            ANY,
            whole((rows, width)),
            whole((rows, width)),
        ]
    )
    return pl.pallas_call(
        functools.partial(
            tail_kernel,
            micros=micros,
            count=count,
            taps=taps,
            clusters=clusters,
            ranks=ranks,
            chunks=chunks,
            states=states,
        ),
        grid_spec=pltpu.PrefetchScalarGridSpec(
            num_scalar_prefetch=1,
            grid=(chunks // 2,),
            in_specs=in_specs,
            out_specs=[whole((extent, width)), whole((extent, width)), whole((rows, width))],
            scratch_shapes=[
                pltpu.VMEM((taps, rows, LANES), F32),
                pltpu.VMEM((rows, LANES), BF16),
                pltpu.VMEM((LANES, cols), BF16),
                pltpu.VMEM((8, own), F32),
                pltpu.VMEM((states * chunks, LANES), F32),
                pltpu.VMEM((rows, width), F32),
                pltpu.VMEM((chunks // 2, 2, LANES, width), BF16),
                pltpu.SemaphoreType.DMA((chunks // 2,)),
                pltpu.VMEM((rows, cols), BF16),
                pltpu.VMEM((LANES, rows), BF16),
                pltpu.VMEM((2 * ranks, rows), BF16),
            ],
        ),
        out_shape=[
            hbm((extent, width), BF16),
            hbm((extent, width), BF16),
            hbm((rows, width), BF16),
        ],
        compiler_params=params(34),
        cost_estimate=cost(7),
        name="tail",
    )(
        place,
        lengths,
        *in_hbm([code_own]),
        code_other,
        *in_hbm(
            (
                sact,
                dpre,
                alog,
                back,
                dtx,
                bc_own,
                bc_other,
                decay,
                bend,
                inner,
                act,
                high,
                convw,
                normed,
                w4,
                gate_part,
                x,
            )
        ),
    )


def fetch_halves(source, which, half, target_ref, sems):
    copies = []
    for k in range(target_ref.shape[0]):
        pair = pl.ds(2 * k, 2)
        block = source.at[pair, half] if which is None else source.at[which, pair, half]
        copies.append(pltpu.make_async_copy(block, target_ref.at[k], sems.at[k]))
    for copy in copies:
        copy.start()
    return copies


def products_kernel(
    place_ref,
    gated_ref,
    dgate_ref,
    out_ref,
    weight_ref,
    mixed_ref,
    dnormed_ref,
    wout_ref,
    wgate_ref,
    out_sems,
    gate_sems,
):
    half = place_ref[HALF]
    width = mixed_ref.shape[1]
    jobs = (
        (fetch_halves(out_ref, None, half, wout_ref, out_sems), gated_ref, wout_ref, mixed_ref),
        (fetch_halves(weight_ref, 1, half, wgate_ref, gate_sems), dgate_ref, wgate_ref, dnormed_ref),
    )
    for copies, left_ref, right_ref, result_ref in jobs:
        total = None
        for k, copy in enumerate(copies):
            copy.wait()
            left = left_ref[:, 2 * k * LANES : 2 * (k + 1) * LANES]
            term = dot(left, right_ref[k].reshape(-1, width), 1, 0)
            total = term if total is None else total + term
        result_ref[...] = total.astype(BF16)


def products(place, gated, dgate, wout3, w4):
    rows, own = gated.shape
    width = w4.shape[-1]
    pairs = own // (2 * LANES)
    return pl.pallas_call(
        products_kernel,
        grid_spec=pltpu.PrefetchScalarGridSpec(
            num_scalar_prefetch=1,
            grid=(1,),
            in_specs=[whole((rows, own)), whole((rows, own)), ANY, ANY],
            out_specs=[whole((rows, width))] * 2,
            scratch_shapes=[
                pltpu.VMEM((pairs, 2, LANES, width), BF16),
                pltpu.VMEM((pairs, 2, LANES, width), BF16),
                pltpu.SemaphoreType.DMA((pairs,)),
                pltpu.SemaphoreType.DMA((pairs,)),
            ],
        ),
        out_shape=[hbm((rows, width), BF16)] * 2,
        compiler_params=params(20),
        cost_estimate=cost(4),
        name="products",
    )(place, *in_hbm((gated, dgate, wout3, w4)))


def finish_kernel(x_ref, mine_ref, theirs_ref, cotan_ref, gain_ref, grad_ref):
    x = x_ref[...].astype(F32)
    scale = lax.rsqrt(jnp.mean(x * x, axis=1, keepdims=True) + EPSILON)
    unit = x * scale
    dhat = (mine_ref[...].astype(F32) + theirs_ref[...].astype(F32)) * gain_ref[...]
    grad_ref[...] = cotan_ref[...].astype(F32) + scale * (
        dhat - unit * jnp.mean(dhat * unit, axis=1, keepdims=True)
    )


def finish(x, mine, theirs, cotan, gain):
    rows, width = x.shape
    by_rows = pl.BlockSpec((rows // 4, width), lambda i: (i, 0))
    return pl.pallas_call(
        finish_kernel,
        grid=(4,),
        in_specs=[by_rows] * 4 + [whole(gain.shape)],
        out_specs=by_rows,
        out_shape=jax.ShapeDtypeStruct((rows, width), F32),
        compiler_params=params(16),
        cost_estimate=cost(0),
        name="finish",
    )(*in_hbm((x, mine)), theirs, *in_hbm((cotan, gain)))


def unpack_kernel(
    near_ref,
    far_ref,
    out_ref,
    dtx_ref,
    dt_ref,
    bc_ref,
    alog_ref,
    convw_ref,
    convb_ref,
    bias_ref,
    skip_ref,
    out_grad_ref,
    *,
    eighth,
    taps,
    edge,
):
    pack = near_ref[...].astype(F32) + far_ref[...].astype(F32)
    turned = jnp.concatenate([pack[:, k * LANES : (k + 1) * LANES] for k in range(4)]).T
    dtx_ref[...] = turned[:edge]
    dt_ref[...] = turned[edge:]
    rows = pack[:, 4 * LANES : 5 * LANES]
    bc_ref[0] = rows[:eighth]
    bc_ref[1] = rows[eighth:]
    rows = pack[:, 5 * LANES : 6 * LANES]
    alog_ref[...] = rows[:eighth]
    vec = rows[eighth:, :edge]
    convw_ref[...] = vec[:taps]
    convb_ref[...] = vec[taps : taps + 1]
    bias_ref[...] = vec[taps + 1 : taps + 2]
    skip_ref[...] = vec[taps + 2 : taps + 3]
    out_grad_ref[...] = out_ref[...].astype(F32)


def unpack(near, far, out, eighth, taps, ranks):
    edge = LANES // 2
    shapes = [
        (edge, ranks),
        (edge, ranks),
        (2, eighth, LANES),
        (eighth, LANES),
        (taps, edge),
        (1, edge),
        (1, edge),
        (1, edge),
        out.shape,
    ]
    return pl.pallas_call(
        functools.partial(unpack_kernel, eighth=eighth, taps=taps, edge=edge),
        grid=(1,),
        in_specs=[whole(array.shape) for array in (near, far, out)],
        out_specs=[whole(shape) for shape in shapes],
        out_shape=[jax.ShapeDtypeStruct(shape, F32) for shape in shapes],
        cost_estimate=cost(0),
        name="unpack",
    )(near, far, out)


def swap_pair(array):
    count = lax.axis_size("state")
    return lax.ppermute(array, "state", [(pos, pos ^ 1) for pos in range(count)])


def swap_bit(array, bits):
    return lax.ppermute(array, "dp", [(pos, pos ^ bits) for pos in range(lax.axis_size("dp"))])


def swap_both(array, bits=0):
    states = lax.axis_size("state")
    pairs = []
    for d in range(lax.axis_size("dp")):
        for s in range(states):
            pairs.append((d * states + s, (((d & ~1) | s) ^ bits) * states + (d & 1)))
    return lax.ppermute(array, ("dp", "state"), pairs)


def add_mixed(x, mine, theirs):
    return (x.astype(F32) + (mine.astype(F32) + theirs.astype(F32))).astype(BF16)


def add_quarters(kept, got, start=0, stop=None):
    extent = kept.shape[0] // 4
    stop = extent if stop is None else stop
    return [
        kept[k * extent + start : k * extent + stop] + got[k * extent + start : k * extent + stop]
        for k in range(4)
    ]


def trade_quarters(quarters):
    return [quarters[0]] + [swap_bit(quarters[k], k * X_BIT) for k in range(1, 4)]


def sum_quarters(quarters):
    left, right = (quarters[k].astype(F32) + quarters[k + 1].astype(F32) for k in (0, 2))
    return (left + right).astype(BF16)


CORE_BIT, X_BIT, ZH_BIT = 1, 2, 8


def shards(
    tokens,
    cluster_len,
    norm_gain,
    in_weight,
    conv_weight,
    conv_bias,
    dtx_weight,
    dt_weight,
    dt_bias,
    bc_weight,
    a_log,
    skip_gain,
    out_weight,
    cotangent,
):
    micros, count, width = tokens.shape
    inner = out_weight.shape[0]
    taps = conv_weight.shape[0]
    ranks = dtx_weight.shape[1]
    chunks = inner // (2 * LANES)
    own = chunks * LANES
    rows = micros * count
    edge = LANES // 2
    span = LANES + 32
    dp_parts = lax.axis_size("dp")
    state_count = lax.axis_size("state")
    dp_pos = lax.axis_index("dp")
    state_pos = lax.axis_index("state")
    half = state_pos & 1
    fast = state_count == 2 and dp_parts == 2 * chunks == 16
    if fast:
        place = jnp.stack([half, dp_pos & 1, dp_pos >> 1, (dp_pos >> 1) & 3])
        bc_own, alog_own = bc_weight, a_log
        bc_other, alog_other = swap_pair(bc_weight), swap_pair(a_log)
    else:
        place = jnp.stack([half, 0, 0, 0])
        bc_all = lax.all_gather(bc_weight, "state", axis=1, tiled=True)
        alog_all = lax.all_gather(a_log, "state", axis=0, tiled=True)
        eighth = alog_all.shape[0] // 2
        bc_own, bc_other = (
            lax.dynamic_slice_in_dim(bc_all, which * eighth, eighth, 1)
            for which in (half, 1 - half)
        )
        alog_own, alog_other = (
            lax.dynamic_slice_in_dim(alog_all, which * eighth, eighth, 0)
            for which in (half, 1 - half)
        )
    place = place.astype(jnp.int32)
    eighth = alog_own.shape[0]
    states = 2 * eighth

    x = tokens.reshape(rows, width)
    cotan = cotangent.reshape(rows, width)
    w4 = in_weight.reshape(2, chunks, 2, LANES, width)
    wout3 = out_weight.reshape(chunks, 2, LANES, width)
    dtx, dt = dtx_weight.T, dt_weight.T
    bias = dt_bias.reshape(-1, LANES)
    skip = skip_gain.reshape(-1, LANES)

    normed, act_all, act, inner_own, bend, gate = project(
        place, cluster_len, x, norm_gain[None], w4, conv_weight, conv_bias.reshape(-1, LANES)
    )
    bc, rank, high, decay, sp, u, step, slope, h, dy, gated, dgate, keep, send = scan_forward(
        place,
        cluster_len,
        act_all,
        bc_own,
        bc_other,
        alog_own,
        alog_other,
        dtx,
        dt,
        bias,
        skip,
        act,
        gate,
        wout3,
        cotan,
        normed,
    )
    if fast:
        early = swap_bit(send, CORE_BIT)
    mixed_part, dn_gate = products(place, gated, dgate, wout3, w4)
    if fast:
        *quarters, mixed_part, dn_gate, sp = lax.optimization_barrier(
            (*add_quarters(keep, early), mixed_part, dn_gate, sp)
        )
        early_got = trade_quarters(quarters)
    code_own, sact, dpre, alog, back = scan_backward(
        place, micros, bc, decay, dt, skip, act, sp, u, step, slope, dy, h
    )
    if fast:
        *early_got, code_own, mixed_part = lax.optimization_barrier(
            (*early_got, code_own, mixed_part)
        )
    code_other = swap_pair(code_own)
    mixed_other = swap_pair(mixed_part)
    if fast:
        block = sum_quarters(early_got)
        out_keep, out_send, gate_sum = block[:edge], block[edge:LANES], block[LANES:]
        out_send, gate_sum, bend = lax.optimization_barrier((out_send, gate_sum, bend))
        out_got = swap_bit(out_send, ZH_BIT)
    late_keep, late_send, dnormed_part = tail(
        place,
        cluster_len,
        code_own,
        code_other,
        sact,
        dpre,
        alog,
        back,
        dtx,
        bc_own,
        bc_other,
        decay,
        bend,
        inner_own,
        act,
        high,
        conv_weight,
        normed,
        w4,
        dn_gate,
        x,
    )
    mixed = add_mixed(x, mixed_part, mixed_other)
    if fast:
        late_send, mixed_other = lax.optimization_barrier((late_send, mixed_other))
        mixed = add_mixed(x, mixed_part, mixed_other)
        late = swap_bit(late_send, CORE_BIT)
        late_got = trade_quarters(add_quarters(late_keep, late))
    dnormed_other = swap_pair(dnormed_part)
    tokens_grad = finish(x, dnormed_part, dnormed_other, cotan, norm_gain[None])
    if fast:
        out_own = swap_both(out_keep + out_got)
        *late_got, out_own, tokens_grad, mixed = lax.optimization_barrier(
            (*late_got, out_own, tokens_grad, mixed)
        )
        block = sum_quarters(late_got)
        inner_sum = block[:LANES]
        upper = dp_pos >= dp_parts // 2
        crossing = jnp.where(upper, inner_sum, gate_sum)
        first, second = crossing[:edge], crossing[edge:]
        first, pack_far, pack_near = lax.optimization_barrier(
            (first, block[-16:], block[LANES:-16])
        )
        pack_far = swap_both(pack_far, ZH_BIT)
        first_got = swap_bit(first, ZH_BIT)
        pack_near = swap_both(pack_near)
        first_got, pack_far, pack_near = lax.optimization_barrier((first_got, pack_far, pack_near))
        second_got = swap_bit(second, ZH_BIT)
        gain_mine = (
            pack_near[:, 5 * LANES : 6 * LANES].astype(F32)
            + pack_far[:, 5 * LANES : 6 * LANES].astype(F32)
        ).astype(BF16)
        gain_both = gain_mine[-1].astype(F32) + swap_bit(gain_mine, CORE_BIT)[-1].astype(F32)
        extent = width // (dp_parts * state_count)
        gain_grad = lax.dynamic_slice_in_dim(gain_both, (dp_pos & 1) * extent, extent, 0)
        (
            dtx_grad,
            dt_grad,
            bc_grad,
            alog_grad,
            convw_grad,
            convb_grad,
            bias_grad,
            skip_grad,
            out_own,
        ) = unpack(pack_near, pack_far, out_own, eighth, taps, ranks)
        convb_grad, bias_grad, skip_grad = (
            array[0] for array in (convb_grad, bias_grad, skip_grad)
        )
        second_got, dtx_grad, dt_grad, out_own = lax.optimization_barrier(
            (second_got, dtx_grad, dt_grad, out_own)
        )
        in_grad = jnp.where(upper, gate_sum, inner_sum).astype(F32) + jnp.concatenate(
            [first_got, second_got]
        ).astype(F32)
    mixed = mixed.reshape(micros, count, width)
    tokens_grad = tokens_grad.reshape(micros, count, width)

    if not fast:
        def total(array):
            return lax.psum(array.astype(F32), "dp")

        def both_rows(array):
            mine = array.reshape(chunks, 1, LANES, -1)
            other = swap_pair(mine)
            low = jnp.where(half == 0, mine, other)
            high = jnp.where(half == 0, other, mine)
            return jnp.concatenate([low, high], axis=1).reshape(2 * own, -1)

        every = dp_parts * state_count
        at = dp_pos * state_count + state_pos

        def cut_own(array):
            extent = array.shape[0] // every
            return lax.dynamic_slice_in_dim(array, at * extent, extent, 0)

        pair = total(jnp.stack([keep, send])).reshape(2, 2, 2, 2 * LANES, width)
        outs = pair[:, :, :, :LANES].reshape(2, 2, 2, 2, edge, width)
        outs = jnp.transpose(outs, (3, 1, 2, 0, 4, 5)).reshape(own, width)
        gates = jnp.moveaxis(pair[:, :, :, LANES:], 0, 2).reshape(own, width)
        pair = total(jnp.stack([late_keep, late_send])).reshape(2, 2, 2, span, width)
        inners = jnp.moveaxis(pair[:, :, :, :LANES], 0, 2).reshape(own, width)
        packs = pair[:, :, :, LANES:].reshape(2, 2, 2, 2, 16, width // LANES, LANES)
        packs = jnp.transpose(packs, (3, 1, 2, 0, 5, 4, 6)).reshape(chunks, 2, -1, 16, LANES)
        small = packs[:, :, :4].reshape(chunks, 2, ranks, 2, edge)
        small = both_rows(jnp.transpose(small, (0, 1, 4, 3, 2)).reshape(own, 2 * ranks))
        in_grad = cut_own(jnp.concatenate([both_rows(inners), both_rows(gates)]))
        out_own = cut_own(both_rows(outs))
        mine = cut_own(small)
        dtx_grad, dt_grad = mine[:, :ranks], mine[:, ranks:]
        vec_rows = jnp.swapaxes(packs[:, :, 5, eighth:, :edge], 2, 3).reshape(own, -1)
        gain_sum = vec_rows[:, -1].reshape(chunks, 2, 2, -1).swapaxes(1, 2).reshape(-1)
        gain_grad = cut_own(gain_sum + swap_pair(gain_sum))
        vec = cut_own(both_rows(vec_rows)).T
        state_rows = jnp.concatenate([packs[:, :, 4], packs[:, :, 5, :eighth]], axis=2)
        state_rows = state_rows.reshape(chunks, 2, 3, eighth, LANES)
        state_rows = jnp.transpose(state_rows, (0, 4, 2, 1, 3)).reshape(own, -1)
        extent = inner // dp_parts
        state_part = lax.dynamic_slice_in_dim(both_rows(state_rows), dp_pos * extent, extent, 0)
        state_part = state_part.T.reshape(3, state_count, -1, extent)
        state_part = lax.dynamic_index_in_dim(state_part, state_pos, 1, keepdims=False)
        bc_grad, alog_grad = state_part[:2], state_part[2]
        convw_grad, convb_grad, bias_grad, skip_grad = (
            vec[:taps], vec[taps], vec[taps + 1], vec[taps + 2]
        )

    return (
        mixed,
        tokens_grad,
        gain_grad,
        in_grad,
        convw_grad,
        convb_grad,
        dtx_grad,
        dt_grad,
        bias_grad,
        bc_grad,
        alog_grad,
        skip_grad,
        out_own,
    )


def solution(mesh):
    return jax.shard_map(
        shards,
        mesh=mesh,
        in_specs=(
            P(None, "dp", None),
            P(None, "dp", None),
            P(),
            P(),
            P(),
            P(),
            P(),
            P(),
            P(),
            P(None, "state", None),
            P("state", None),
            P(),
            P(),
            P(None, "dp", None),
        ),
        out_specs=(
            P(None, "dp", None),
            P(None, "dp", None),
            P(("dp", "state")),
            P(("dp", "state"), None),
            P(None, ("dp", "state")),
            P(("dp", "state")),
            P(("dp", "state"), None),
            P(("dp", "state"), None),
            P(("dp", "state")),
            P(None, "state", "dp"),
            P("state", "dp"),
            P(("dp", "state")),
            P(("dp", "state"), None),
        ),
        check_vma=False,
    )
```

profile of v0, /device:TPU:1, one launch (start us, length us, event | category | flops | bytes accessed | tf_op | source)
XLA Modules:
  0.0 121.6 jit_solution(8754866270734887515)
XLA Ops:
  0.6 2.1 %collective-permute-start.1 = (f32[8,2048]{1,0:T(8,128)}, f32[8,2048]{1,0:T(8,128)S(1)}, u32[]{:S(2)}, u32[]{:S(2)}) collective-permute-start(f32[8,2048]{1,0:T(8,128)} %alog_own_ref.1), channel_id=1, source_target_pairs={{0,1},{1,0},{2,3},{3,2},{4,5},{5,4},{6,7},{7,6},{8,9},{9,8},{10,11... | collective-permute-start | bytes 196616 | tf_op jit(solution)/shard_map/ppermute | solution.py:1148
  2.9 9.0 %project.1 = (bf16[256,1024]{1,0:T(8,128)(2,1)}, bf16[256,2048]{1,0:T(8,128)(2,1)}, bf16[256,1024]{1,0:T(8,128)(2,1)}, f32[256,1024]{1,0:T(8,128)}, bf16[256,1024]{1,0:T(8,128)(2,1)}, /*index=5*/f32[256,1024]{1,0:T(8,128)}) custom-call(s32[4]{0:T(128)S(1)} %pad_add_fusion.place_ref, s32[2,1,2]{2,1,0:T(1,128)} %len_ref.5, f32[1,1024]{1,0:T(1,128)} %bitcast.33, ...), custom_call_target="tpu_custom_call" | custom-call | flops 6000000000 | bytes 6000000 | tf_op jit(solution)/shard_map/project/pallas_call | solution.py:211
  12.0 16.0 %scan_forward.1 = (f32[256,32]{1,0:T(8,128)}, bf16[256,64]{1,0:T(8,128)(2,1)}, bf16[256,128]{1,0:T(8,128)(2,1)}, f32[128,128]{1,0:T(8,128)}, f32[2048,128]{1,0:T...) custom-call(s32[4]{0:T(128)S(1)} %pad_add_fusion.place_ref, ...), custom_call_target="tpu_custom_call" | custom-call | flops 19000000512 | bytes 19000000 | tf_op jit(solution)/shard_map/scan_forward/pallas_call | solution.py:465
  29.1 5.8 %products.1 = (bf16[256,1024]{1,0:T(8,128)(2,1)}, bf16[256,1024]{1,0:T(8,128)(2,1)}) custom-call(s32[4]{0:T(128)S(1)} %pad_add_fusion.place_ref, bf16[256,1024]{1,0:T(8,128)(2,1)} %get-tuple-element.92.gated_ref, bf16[256,1024]{1,0:T(8,128)(2,1)} %get-tuple-element.93.dgate_ref, bf16[8,2,128,1024]{3,2,1,0:T(8,128)(2,1)} %bitcast.39, ...), custom_call_target="tpu_custom_call" | custom-call | flops 4000000000 | bytes 4000000 | tf_op jit(solution)/shard_map/products/pallas_call | solution.py:1041
  35.2 1.7 %collective-permute-start.3 = (bf16[256,1024]{1,0:T(8,128)(2,1)S(1)}, bf16[256,1024]{1,0:T(8,128)(2,1)S(1)}, u32[]{:S(2)}, u32[]{:S(2)}) collective-permute-start(bf16[256,1024]{1,0:T(8,128)(2,1)S(1)} %get-tuple-element.98), channel_id=1, source_target_pairs={{0,4},{2,6},{4,0},{6,2},{8,12},{10,14},{12,8},{14,10},{16,20},{18,... | collective-permute-start | bytes 1572872 | tf_op jit(solution)/shard_map/ppermute | solution.py:1152
  36.9 1.3 %collective-permute-start.4 = (bf16[256,1024]{1,0:T(8,128)(2,1)S(1)}, bf16[256,1024]{1,0:T(8,128)(2,1)S(1)}, u32[]{:S(2)}, u32[]{:S(2)}) collective-permute-start(bf16[256,1024]{1,0:T(8,128)(2,1)S(1)} %get-tuple-element.99), channel_id=1, source_target_pairs={{0,8},{2,10},{4,12},{6,14},{8,0},{10,2},{12,4},{14,6},{16,24},{18,... | collective-permute-start | bytes 1572872 | tf_op jit(solution)/shard_map/ppermute | solution.py:1152
  38.2 24.4 %scan_backward.1 = (bf16[256,128]{1,0:T(8,128)(2,1)}, f32[256,1024]{1,0:T(8,128)}, bf16[256,1024]{1,0:T(8,128)(2,1)}, f32[128,128]{1,0:T(8,128)}, f32[2,1024]{1,0:T(2,128)}) custom-call(s32[4]{0:T(128)S(1)} %pad_add_fusion.place_ref, f32[256,32]{1,0:T(8,128)} %get-tuple-element.101.bc_ref, f32[128,128]{1,0:T(8,128)} %get-tuple-element.102.decay_ref.refs_9_, ...), custom_call_target="tpu_custom_call" | custom-call | tf_op jit(solution)/shard_map/scan_backward/pallas_call | solution.py:690
  62.7 1.4 %collective-permute-start.6 = (bf16[256,128]{1,0:T(8,128)(2,1)}, bf16[256,128]{1,0:T(8,128)(2,1)S(1)}, u32[]{:S(2)}, u32[]{:S(2)}) collective-permute-start(bf16[256,128]{1,0:T(8,128)(2,1)} %get-tuple-element.111.refs_0_), channel_id=1, source_target_pairs={{0,1},{1,0},{2,3},{3,2},{4,5},{5,4},{6,7},{7,6},{8,9},{9,8},{10,11... | collective-permute-start | bytes 196616 | tf_op jit(solution)/shard_map/ppermute | solution.py:1148
  66.0 10.3 %tail.1 = (bf16[640,1024]{1,0:T(8,128)(2,1)}, bf16[640,1024]{1,0:T(8,128)(2,1)}, bf16[256,1024]{1,0:T(8,128)(2,1)}) custom-call(s32[4]{0:T(128)S(1)} %pad_add_fusion.place_ref, s32[2,1,2]{2,1,0:T(1,128)S(1)} %copy-done.3, bf16[256,128]{1,0:T(8,128)(2,1)} %get-tuple-element.111.refs_0_, bf16[256,128]{1,0:T(8,128)(2,1)S(1)} %collective-permute-done.6.refs_1_, ...), custom_call_target="tpu_custom_call" | custom-call | flops 7000000000 | bytes 7000000 | tf_op jit(solution)/shard_map/tail/pallas_call | solution.py:930
  77.0 2.0 %collective-permute-start.8 = (bf16[640,1024]{1,0:T(8,128)(2,1)}, bf16[640,1024]{1,0:T(8,128)(2,1)S(1)}, u32[]{:S(2)}, u32[]{:S(2)}) collective-permute-start(bf16[640,1024]{1,0:T(8,128)(2,1)} %get-tuple-element.128), channel_id=1, source_target_pairs={{0,2},{2,0},{4,6},{6,4},{8,10},{10,8},{12,14},{14,12},{16,18},{18,... | collective-permute-start | bytes 3932168 | tf_op jit(solution)/shard_map/ppermute | solution.py:1152
  79.0 2.7 %collective-permute-start.12 = (bf16[64,1024]{1,0:T(8,128)(2,1)S(1)}, bf16[64,1024]{1,0:T(8,128)(2,1)S(1)}, u32[]{:S(2)}, u32[]{:S(2)}) collective-permute-start(bf16[64,1024]{1,0:T(8,128)(2,1)S(1)} %slice.116), channel_id=1, source_target_pairs={{0,16},{2,18},{4,20},{6,22},{8,24},{10,26},{12,28},{14,30},{16,0},... | collective-permute-start | bytes 393224 | tf_op jit(solution)/shard_map/ppermute | solution.py:1152
  82.8 1.5 %slice_add_fusion.4 = (bf16[160,1024]{1,0:T(8,128)(2,1)S(1)}, bf16[160,1024]{1,0:T(8,128)(2,1)S(1)}, bf16[160,1024]{1,0:T(8,128)(2,1)S(1)}, bf16[160,1024]{1,0:T(8,128)(2,1)S(1)}) fusion(bf16[640,1024]{1,0:T(8,128)(2,1)S(1)} %collective-permute-done.8, bf16[640,1024]{1,0:T(8,128)(2,1)} %get-tuple-element.125), kind=kLoop, calls=%fused_computation.8 | loop fusion | flops 655360 | bytes 3932160 | tf_op jit(solution)/shard_map/add | solution.py:1172
  84.2 2.3 %collective-permute-start.11 = (bf16[160,1024]{1,0:T(8,128)(2,1)S(1)}, bf16[160,1024]{1,0:T(8,128)(2,1)S(1)}, u32[]{:S(2)}, u32[]{:S(2)}) collective-permute-start(bf16[160,1024]{1,0:T(8,128)(2,1)S(1)} %get-tuple-element.163), channel_id=1, source_target_pairs={{0,12},{2,14},{4,8},{6,10},{8,4},{10,6},{12,0},{14,2},{16,28},{18,... | collective-permute-start | bytes 983048 | tf_op jit(solution)/shard_map/ppermute | solution.py:1152
  86.9 1.5 %collective-permute-done.12 = bf16[64,1024]{1,0:T(8,128)(2,1)S(1)} collective-permute-done((bf16[64,1024]{1,0:T(8,128)(2,1)S(1)}, bf16[64,1024]{1,0:T(8,128)(2,1)S(1)}, u32[]{:S(2)}, u32[]{:S(2)}) %collective-permute-start.12) | collective-permute-done | bytes 131104 | tf_op jit(solution)/shard_map/ppermute | solution.py:1152
  88.4 3.6 %collective-permute-start.13 = (bf16[64,1024]{1,0:T(8,128)(2,1)S(1)}, bf16[64,1024]{1,0:T(8,128)(2,1)S(1)}, u32[]{:S(2)}, u32[]{:S(2)}) collective-permute-start(bf16[64,1024]{1,0:T(8,128)(2,1)S(1)} %slice_add_fusion.8), channel_id=1, source_target_pairs={{0,0},{1,2},{2,1},{3,3},{4,4},{5,6},{6,5},{7,7},{8,8},{9,10},{10,9... | collective-permute-start | bytes 393224 | tf_op jit(solution)/shard_map/ppermute | solution.py:1161
  93.1 2.1 %collective-permute-done.14.theirs_ref = bf16[256,1024]{1,0:T(8,128)(2,1)S(1)} collective-permute-done((bf16[256,1024]{1,0:T(8,128)(2,1)}, bf16[256,1024]{1,0:T(8,128)(2,1)S(1)}, u32[]{:S(2)}, u32[]{:S(2)}) %collective-permute-start.14) | collective-permute-done | bytes 524320 | tf_op jit(solution)/shard_map/ppermute | solution.py:1148
  95.2 3.9 %finish.1 = f32[256,1024]{1,0:T(8,128)} custom-call(bf16[256,1024]{1,0:T(8,128)(2,1)} %bitcast.24, bf16[256,1024]{1,0:T(8,128)(2,1)} %get-tuple-element.130.mine_ref, bf16[256,1024]{1,0:T(8,128)(2,1)S(1)} %collective-permute-done.14.theirs_ref, bf16[256,1024]{1,0:T(8,128)(2,1)} %bitcast.27, f32[1,1024]{1,0:T(1,128)} %bitcast.34), custom_call_target="tpu_custom_call" | custom-call | tf_op jit(solution)/shard_map/finish/pallas_call | solution.py:1075
  99.1 3.1 %collective-permute-done.10 = bf16[160,1024]{1,0:T(8,128)(2,1)S(1)} collective-permute-done((bf16[160,1024]{1,0:T(8,128)(2,1)S(1)}, bf16[160,1024]{1,0:T(8,128)(2,1)S(1)}, u32[]{:S(2)}, u32[]{:S(2)}) %collective-permute-start.10) | collective-permute-done | bytes 327712 | tf_op jit(solution)/shard_map/ppermute | solution.py:1152
  103.2 1.1 collective-permute-start.15
  104.3 2.5 %collective-permute-start.16 = (bf16[16,1024]{1,0:T(8,128)(2,1)S(1)}, bf16[16,1024]{1,0:T(8,128)(2,1)S(1)}, u32[]{:S(2)}, u32[]{:S(2)}) collective-permute-start(bf16[16,1024]{1,0:T(8,128)(2,1)S(1)} %get-tuple-element.140), channel_id=1, source_target_pairs={{0,16},{1,18},{2,17},{3,19},{4,20},{5,22},{6,21},{7,23},{8,24},{9,... | collective-permute-start | bytes 98312 | tf_op jit(solution)/shard_map/ppermute | solution.py:1161
  106.8 2.2 %collective-permute-start.17 = (bf16[16,1024]{1,0:T(8,128)(2,1)S(1)}, bf16[16,1024]{1,0:T(8,128)(2,1)S(1)}, u32[]{:S(2)}, u32[]{:S(2)}) collective-permute-start(bf16[16,1024]{1,0:T(8,128)(2,1)S(1)} %get-tuple-element.141), channel_id=1, source_target_pairs={{0,0},{1,2},{2,1},{3,3},{4,4},{5,6},{6,5},{7,7},{8,8},{9,10},{10,9... | collective-permute-start | bytes 98312 | tf_op jit(solution)/shard_map/ppermute | solution.py:1161
  109.0 1.1 collective-permute-start.19
  110.1 7.7 %collective-permute-done.16.far_ref = bf16[16,1024]{1,0:T(8,128)(2,1)S(1)} collective-permute-done((bf16[16,1024]{1,0:T(8,128)(2,1)S(1)}, bf16[16,1024]{1,0:T(8,128)(2,1)S(1)}, u32[]{:S(2)}, u32[]{:S(2)}) %collective-permute-start.16) | collective-permute-done | bytes 32800 | tf_op jit(solution)/shard_map/ppermute | solution.py:1161
  118.4 1.7 %unpack.1 = (f32[64,64]{1,0:T(8,128)}, f32[64,64]{1,0:T(8,128)}, f32[2,8,128]{2,1,0:T(8,128)}, f32[8,128]{1,0:T(8,128)}, f32[4,64]{1,0:T(4,128)}, /*index=5*/f32...) custom-call(bf16[16,1024]{1,0:T(8,128)(2,1)} %copy-done.9, bf16[16,1024]{1,0:T(8,128)(2,1)} %copy-done.8, ...), custom_call_target="tpu_custom_call" | custom-call | tf_op jit(solution)/shard_map/unpack/pallas_call | solution.py:1135
  (59 shorter events, 9.6 us)
Async XLA Ops:
  0.6 11.3 %collective-permute-start.1 = (f32[8,2048]{1,0:T(8,128)}, f32[8,2048]{1,0:T(8,128)S(1)}, u32[]{:S(2)}, u32[]{:S(2)}) collective-permute-start(f32[8,2048]{1,0:T(8,128)} %alog_own_ref.1), channel_id=1, source_target_pairs={{0,1},{1,0},{2,3},{3,2},{4,5},{5,4},{6,7},{7,6},{8,9},{9,8},{10,11... | collective-permute-start | bytes 196616 | tf_op jit(solution)/shard_map/ppermute | solution.py:1148
  2.8 9.2 %collective-permute-start = (bf16[2,8,2048]{2,1,0:T(8,128)(2,1)}, bf16[2,8,2048]{2,1,0:T(8,128)(2,1)S(1)}, u32[]{:S(2)}, u32[]{:S(2)}) collective-permute-start(bf16[2,8,2048]{2,1,0:T(8,128)(2,1)} %refs_7_.1), channel_id=1, source_target_pairs={{0,1},{1,0},{2,3},{3,2},{4,5},{5,4},{6,7},{7,6},{8,9},{9,8},{10,11... | collective-permute-start | bytes 196616 | tf_op jit(solution)/shard_map/ppermute | solution.py:1148
  2.9 9.1 %copy-start.3 = (s32[2,1,2]{2,1,0:T(1,128)S(1)}, s32[2,1,2]{2,1,0:T(1,128)}, u32[]{:S(2)}) copy-start(s32[2,1,2]{2,1,0:T(1,128)} %len_ref.5) | copy-start | bytes 52
  12.0 16.1 %copy-start.2 = (bf16[2,8,2048]{2,1,0:T(8,128)(2,1)}, bf16[2,8,2048]{2,1,0:T(8,128)(2,1)S(1)}, u32[]{:S(2)}) copy-start(bf16[2,8,2048]{2,1,0:T(8,128)(2,1)S(1)} %collective-permute-done.bc_other_ref.refs_8_) | copy-start | bytes 196612
  28.1 6.9 %collective-permute-start.2 = (bf16[1024,1024]{1,0:T(8,128)(2,1)}, bf16[1024,1024]{1,0:T(8,128)(2,1)S(1)}, u32[]{:S(2)}, u32[]{:S(2)}) collective-permute-start(bf16[1024,1024]{1,0:T(8,128)(2,1)} %get-tuple-element.91), channel_id=1, source_target_pairs={{0,2},{2,0},{4,6},{6,4},{8,10},{10,8},{12,14},{14,12},{16,18},{18,... | collective-permute-start | bytes 6291464 | tf_op jit(solution)/shard_map/ppermute | solution.py:1152
  35.2 27.4 %collective-permute-start.3 = (bf16[256,1024]{1,0:T(8,128)(2,1)S(1)}, bf16[256,1024]{1,0:T(8,128)(2,1)S(1)}, u32[]{:S(2)}, u32[]{:S(2)}) collective-permute-start(bf16[256,1024]{1,0:T(8,128)(2,1)S(1)} %get-tuple-element.98), channel_id=1, source_target_pairs={{0,4},{2,6},{4,0},{6,2},{8,12},{10,14},{12,8},{14,10},{16,20},{18,... | collective-permute-start | bytes 1572872 | tf_op jit(solution)/shard_map/ppermute | solution.py:1152
  36.9 25.8 %collective-permute-start.4 = (bf16[256,1024]{1,0:T(8,128)(2,1)S(1)}, bf16[256,1024]{1,0:T(8,128)(2,1)S(1)}, u32[]{:S(2)}, u32[]{:S(2)}) collective-permute-start(bf16[256,1024]{1,0:T(8,128)(2,1)S(1)} %get-tuple-element.99), channel_id=1, source_target_pairs={{0,8},{2,10},{4,12},{6,14},{8,0},{10,2},{12,4},{14,6},{16,24},{18,... | collective-permute-start | bytes 1572872 | tf_op jit(solution)/shard_map/ppermute | solution.py:1152
  38.2 24.5 %collective-permute-start.5 = (bf16[256,1024]{1,0:T(8,128)(2,1)S(1)}, bf16[256,1024]{1,0:T(8,128)(2,1)S(1)}, u32[]{:S(2)}, u32[]{:S(2)}) collective-permute-start(bf16[256,1024]{1,0:T(8,128)(2,1)S(1)} %get-tuple-element.100), channel_id=1, source_target_pairs={{0,12},{2,14},{4,8},{6,10},{8,4},{10,6},{12,0},{14,2},{16,28},{18,... | collective-permute-start | bytes 1572872 | tf_op jit(solution)/shard_map/ppermute | solution.py:1152
  62.7 3.4 %collective-permute-start.6 = (bf16[256,128]{1,0:T(8,128)(2,1)}, bf16[256,128]{1,0:T(8,128)(2,1)S(1)}, u32[]{:S(2)}, u32[]{:S(2)}) collective-permute-start(bf16[256,128]{1,0:T(8,128)(2,1)} %get-tuple-element.111.refs_0_), channel_id=1, source_target_pairs={{0,1},{1,0},{2,3},{3,2},{4,5},{5,4},{6,7},{7,6},{8,9},{9,8},{10,11... | collective-permute-start | bytes 196616 | tf_op jit(solution)/shard_map/ppermute | solution.py:1148
  64.5 12.5 %collective-permute-start.7 = (bf16[256,1024]{1,0:T(8,128)(2,1)S(1)}, bf16[256,1024]{1,0:T(8,128)(2,1)S(1)}, u32[]{:S(2)}, u32[]{:S(2)}) collective-permute-start(bf16[256,1024]{1,0:T(8,128)(2,1)S(1)} %copy-done.6), channel_id=1, source_target_pairs={{0,1},{1,0},{2,3},{3,2},{4,5},{5,4},{6,7},{7,6},{8,9},{9,8},{10,11... | collective-permute-start | bytes 1572872 | tf_op jit(solution)/shard_map/ppermute | solution.py:1148
  77.0 5.7 %collective-permute-start.8 = (bf16[640,1024]{1,0:T(8,128)(2,1)}, bf16[640,1024]{1,0:T(8,128)(2,1)S(1)}, u32[]{:S(2)}, u32[]{:S(2)}) collective-permute-start(bf16[640,1024]{1,0:T(8,128)(2,1)} %get-tuple-element.128), channel_id=1, source_target_pairs={{0,2},{2,0},{4,6},{6,4},{8,10},{10,8},{12,14},{14,12},{16,18},{18,... | collective-permute-start | bytes 3932168 | tf_op jit(solution)/shard_map/ppermute | solution.py:1152
  79.0 9.4 %collective-permute-start.12 = (bf16[64,1024]{1,0:T(8,128)(2,1)S(1)}, bf16[64,1024]{1,0:T(8,128)(2,1)S(1)}, u32[]{:S(2)}, u32[]{:S(2)}) collective-permute-start(bf16[64,1024]{1,0:T(8,128)(2,1)S(1)} %slice.116), channel_id=1, source_target_pairs={{0,16},{2,18},{4,20},{6,22},{8,24},{10,26},{12,28},{14,30},{16,0},... | collective-permute-start | bytes 393224 | tf_op jit(solution)/shard_map/ppermute | solution.py:1152
  81.7 13.4 %collective-permute-start.14 = (bf16[256,1024]{1,0:T(8,128)(2,1)}, bf16[256,1024]{1,0:T(8,128)(2,1)S(1)}, u32[]{:S(2)}, u32[]{:S(2)}) collective-permute-start(bf16[256,1024]{1,0:T(8,128)(2,1)} %get-tuple-element.130.mine_ref), channel_id=1, source_target_pairs={{0,1},{1,0},{2,3},{3,2},{4,5},{5,4},{6,7},{7,6},{8,9},{9,8},{10,11... | collective-permute-start | bytes 1572872 | tf_op jit(solution)/shard_map/ppermute | solution.py:1148
  82.8 9.2 %copy-start.5 = (bf16[2,128,1024]{2,1,0:T(8,128)(2,1)S(1)}, bf16[2,128,1024]{2,1,0:T(8,128)(2,1)}, u32[]{:S(2)}) copy-start(bf16[2,128,1024]{2,1,0:T(8,128)(2,1)} %param.14) | copy-start | bytes 1572868
  84.2 14.9 %collective-permute-start.11 = (bf16[160,1024]{1,0:T(8,128)(2,1)S(1)}, bf16[160,1024]{1,0:T(8,128)(2,1)S(1)}, u32[]{:S(2)}, u32[]{:S(2)}) collective-permute-start(bf16[160,1024]{1,0:T(8,128)(2,1)S(1)} %get-tuple-element.163), channel_id=1, source_target_pairs={{0,12},{2,14},{4,8},{6,10},{8,4},{10,6},{12,0},{14,2},{16,28},{18,... | collective-permute-start | bytes 983048 | tf_op jit(solution)/shard_map/ppermute | solution.py:1152
  86.5 15.8 %collective-permute-start.10 = (bf16[160,1024]{1,0:T(8,128)(2,1)S(1)}, bf16[160,1024]{1,0:T(8,128)(2,1)S(1)}, u32[]{:S(2)}, u32[]{:S(2)}) collective-permute-start(bf16[160,1024]{1,0:T(8,128)(2,1)S(1)} %get-tuple-element.164), channel_id=1, source_target_pairs={{0,8},{2,10},{4,12},{6,14},{8,0},{10,2},{12,4},{14,6},{16,24},{18,... | collective-permute-start | bytes 983048 | tf_op jit(solution)/shard_map/ppermute | solution.py:1152
  86.7 16.2 %collective-permute-start.9 = (bf16[160,1024]{1,0:T(8,128)(2,1)S(1)}, bf16[160,1024]{1,0:T(8,128)(2,1)S(1)}, u32[]{:S(2)}, u32[]{:S(2)}) collective-permute-start(bf16[160,1024]{1,0:T(8,128)(2,1)S(1)} %get-tuple-element.165), channel_id=1, source_target_pairs={{0,4},{2,6},{4,0},{6,2},{8,12},{10,14},{12,8},{14,10},{16,20},{18,... | collective-permute-start | bytes 983048 | tf_op jit(solution)/shard_map/ppermute | solution.py:1152
  88.4 10.7 %collective-permute-start.13 = (bf16[64,1024]{1,0:T(8,128)(2,1)S(1)}, bf16[64,1024]{1,0:T(8,128)(2,1)S(1)}, u32[]{:S(2)}, u32[]{:S(2)}) collective-permute-start(bf16[64,1024]{1,0:T(8,128)(2,1)S(1)} %slice_add_fusion.8), channel_id=1, source_target_pairs={{0,0},{1,2},{2,1},{3,3},{4,4},{5,6},{6,5},{7,7},{8,8},{9,10},{10,9... | collective-permute-start | bytes 393224 | tf_op jit(solution)/shard_map/ppermute | solution.py:1161
  99.1 18.8 %copy-start.7 = (bf16[64,1024]{1,0:T(8,128)(2,1)}, bf16[64,1024]{1,0:T(8,128)(2,1)S(1)}, u32[]{:S(2)}) copy-start(bf16[64,1024]{1,0:T(8,128)(2,1)S(1)} %collective-permute-done.13.out_ref) | copy-start | bytes 393220
  103.2 14.6 %collective-permute-start.15 = (bf16[64,1024]{1,0:T(8,128)(2,1)S(1)}, bf16[64,1024]{1,0:T(8,128)(2,1)S(1)}, u32[]{:S(2)}, u32[]{:S(2)}) collective-permute-start(bf16[64,1024]{1,0:T(8,128)(2,1)S(1)} %get-tuple-element.139), channel_id=1, source_target_pairs={{0,16},{2,18},{4,20},{6,22},{8,24},{10,26},{12,28},{14,30},{16,0},... | collective-permute-start | bytes 393224 | tf_op jit(solution)/shard_map/ppermute | solution.py:1152
  104.3 13.5 %collective-permute-start.16 = (bf16[16,1024]{1,0:T(8,128)(2,1)S(1)}, bf16[16,1024]{1,0:T(8,128)(2,1)S(1)}, u32[]{:S(2)}, u32[]{:S(2)}) collective-permute-start(bf16[16,1024]{1,0:T(8,128)(2,1)S(1)} %get-tuple-element.140), channel_id=1, source_target_pairs={{0,16},{1,18},{2,17},{3,19},{4,20},{5,22},{6,21},{7,23},{8,24},{9,... | collective-permute-start | bytes 98312 | tf_op jit(solution)/shard_map/ppermute | solution.py:1161
  106.8 11.1 %collective-permute-start.17 = (bf16[16,1024]{1,0:T(8,128)(2,1)S(1)}, bf16[16,1024]{1,0:T(8,128)(2,1)S(1)}, u32[]{:S(2)}, u32[]{:S(2)}) collective-permute-start(bf16[16,1024]{1,0:T(8,128)(2,1)S(1)} %get-tuple-element.141), channel_id=1, source_target_pairs={{0,0},{1,2},{2,1},{3,3},{4,4},{5,6},{6,5},{7,7},{8,8},{9,10},{10,9... | collective-permute-start | bytes 98312 | tf_op jit(solution)/shard_map/ppermute | solution.py:1161
  109.0 11.1 %collective-permute-start.19 = (bf16[64,1024]{1,0:T(8,128)(2,1)S(1)}, bf16[64,1024]{1,0:T(8,128)(2,1)S(1)}, u32[]{:S(2)}, u32[]{:S(2)}) collective-permute-start(bf16[64,1024]{1,0:T(8,128)(2,1)S(1)} %get-tuple-element.169), channel_id=1, source_target_pairs={{0,16},{2,18},{4,20},{6,22},{8,24},{10,26},{12,28},{14,30},{16,0},... | collective-permute-start | bytes 393224 | tf_op jit(solution)/shard_map/ppermute | solution.py:1152
  117.8 3.2 %collective-permute-start.18 = (bf16[16,128]{1,0:T(8,128)(2,1)S(1)}, bf16[16,128]{1,0:T(8,128)(2,1)S(1)}, u32[]{:S(2)}, u32[]{:S(2)}) collective-permute-start(bf16[16,128]{1,0:T(8,128)(2,1)S(1)} %add_convert_fusion.3), channel_id=1, source_target_pairs={{0,2},{2,0},{4,6},{6,4},{8,10},{10,8},{12,14},{14,12},{16,18},{18,... | collective-permute-start | bytes 12296 | tf_op jit(solution)/shard_map/ppermute | solution.py:1152
  (6 other events, 27.1 us)
where the time goes:
time: 122 us
  Pallas kernels  71.2 us (58%)
  starting transfers between devices  27.2 us (22%)
  waiting for transfers between devices  16.7 us (14%)
  other arithmetic  4.38 us (4%)
    pallas_call x1, Pallas kernels, scan_backward(): pl.pallas_call(functools.partial(backward_kernel, count=count, states=sta...  24.4 us
    pallas_call x1, Pallas kernels, scan_forward(): pl.pallas_call(functools.partial(forward_kernel, micros=micros, count=row...  16 us
    ppermute x12, starting transfers between devices, swap_bit(): lax.ppermute(array, 'dp', [(pos, pos ^ bits) for pos in range(lax.axis_si...  13.8 us
    pallas_call x1, Pallas kernels, tail(): pl.pallas_call(functools.partial(tail_kernel, micros=micros, count=count,...  10.3 us
    pallas_call x1, Pallas kernels, project(): pl.pallas_call(functools.partial(project_kernel, micros=micros, count=row...  9.04 us
    ppermute x3, starting transfers between devices, swap_both(): return lax.ppermute(array, ('dp', 'state'), pairs)  8.2 us
    ppermute x3, waiting for transfers between devices, swap_both(): return lax.ppermute(array, ('dp', 'state'), pairs)  7.7 us
    pallas_call x1, Pallas kernels, products(): pl.pallas_call(products_kernel, grid_spec=pltpu.PrefetchScalarGridSpec(nu...  5.83 us
  transfers between devices with their start and end apart: 20, of which 7 were waited for; matrix products, arithmetic and copies ran while one was open for 3% of the time, Pallas kernels for 45%

commit v1 on v0

--- a/solution.py
+++ b/solution.py
@@ -585,8 +585,8 @@
 
     def retreat(back, carry):
         flows, totals = carry
-        for slot in range(4):
-            t = count - 1 - (4 * back + slot)
+        for slot in range(8):
+            t = count - 1 - (8 * back + slot)
             span = pl.ds(t, chunks, stride=count)
             sp = sp_ref[span, :]
             u = u_ref[span, :]
@@ -620,7 +620,7 @@
     carry = (zero, zero)
     for k in range(SEGMENTS):
         fetch(micro, SEGMENTS - 1 - k).wait()
-        carry = lax.fori_loop(k * segment // 4, (k + 1) * segment // 4, retreat, carry)
+        carry = lax.fori_loop(k * segment // 8, (k + 1) * segment // 8, retreat, carry)
     totals = carry[1]
     for n in range(states):
         alog_ref[pl.ds(n * chunks, chunks), :] += totals[n]

time: 122 us -> 123 us (level)
  transfers between devices with their start and end apart: 20 -> 20, of which waited for: 7 -> 7; matrix products, arithmetic and copies ran while one was open for 3% -> 3% of each run, Pallas kernels for 45% -> 46%
where the time goes in v1:
time: 123 us
  Pallas kernels  72.4 us (59%)
  starting transfers between devices  27.2 us (22%)
  waiting for transfers between devices  16.7 us (14%)
  other arithmetic  4.38 us (4%)
    pallas_call x1, Pallas kernels, scan_backward(): pl.pallas_call(functools.partial(backward_kernel, count=count, states=sta...  25.3 us
    pallas_call x1, Pallas kernels, scan_forward(): pl.pallas_call(functools.partial(forward_kernel, micros=micros, count=row...  16 us
    ppermute x12, starting transfers between devices, swap_bit(): lax.ppermute(array, 'dp', [(pos, pos ^ bits) for pos in range(lax.axis_si...  12.9 us
    pallas_call x1, Pallas kernels, tail(): pl.pallas_call(functools.partial(tail_kernel, micros=micros, count=count,...  10.5 us
    pallas_call x1, Pallas kernels, project(): pl.pallas_call(functools.partial(project_kernel, micros=micros, count=row...  9.04 us
    ppermute x3, starting transfers between devices, swap_both(): return lax.ppermute(array, ('dp', 'state'), pairs)  8.95 us
    ppermute x3, waiting for transfers between devices, swap_both(): return lax.ppermute(array, ('dp', 'state'), pairs)  7.77 us
    pallas_call x1, Pallas kernels, products(): pl.pallas_call(products_kernel, grid_spec=pltpu.PrefetchScalarGridSpec(nu...  5.83 us
  transfers between devices with their start and end apart: 20, of which 7 were waited for; matrix products, arithmetic and copies ran while one was open for 3% of the time, Pallas kernels for 46%

profile of v1, /device:TPU:1, one launch (start us, length us, event | category | flops | bytes accessed | tf_op | source)
XLA Modules:
  0.0 122.8 jit_solution(11396824930618325926)
XLA Ops:
  0.6 2.1 %collective-permute-start.1 = (f32[8,2048]{1,0:T(8,128)}, f32[8,2048]{1,0:T(8,128)S(1)}, u32[]{:S(2)}, u32[]{:S(2)}) collective-permute-start(f32[8,2048]{1,0:T(8,128)} %alog_own_ref.1), channel_id=1, source_target_pairs={{0,1},{1,0},{2,3},{3,2},{4,5},{5,4},{6,7},{7,6},{8,9},{9,8},{10,11... | collective-permute-start | bytes 196616 | tf_op jit(solution)/shard_map/ppermute | solution.py:1148
  2.9 9.0 %project.1 = (bf16[256,1024]{1,0:T(8,128)(2,1)}, bf16[256,2048]{1,0:T(8,128)(2,1)}, bf16[256,1024]{1,0:T(8,128)(2,1)}, f32[256,1024]{1,0:T(8,128)}, bf16[256,1024]{1,0:T(8,128)(2,1)}, /*index=5*/f32[256,1024]{1,0:T(8,128)}) custom-call(s32[4]{0:T(128)S(1)} %pad_add_fusion.place_ref, s32[2,1,2]{2,1,0:T(1,128)} %len_ref.5, f32[1,1024]{1,0:T(1,128)} %bitcast.33, ...), custom_call_target="tpu_custom_call" | custom-call | flops 6000000000 | bytes 6000000 | tf_op jit(solution)/shard_map/project/pallas_call | solution.py:211
  12.0 16.0 %scan_forward.1 = (f32[256,32]{1,0:T(8,128)}, bf16[256,64]{1,0:T(8,128)(2,1)}, bf16[256,128]{1,0:T(8,128)(2,1)}, f32[128,128]{1,0:T(8,128)}, f32[2048,128]{1,0:T...) custom-call(s32[4]{0:T(128)S(1)} %pad_add_fusion.place_ref, ...), custom_call_target="tpu_custom_call" | custom-call | flops 19000000512 | bytes 19000000 | tf_op jit(solution)/shard_map/scan_forward/pallas_call | solution.py:465
  29.1 5.8 %products.1 = (bf16[256,1024]{1,0:T(8,128)(2,1)}, bf16[256,1024]{1,0:T(8,128)(2,1)}) custom-call(s32[4]{0:T(128)S(1)} %pad_add_fusion.place_ref, bf16[256,1024]{1,0:T(8,128)(2,1)} %get-tuple-element.92.gated_ref, bf16[256,1024]{1,0:T(8,128)(2,1)} %get-tuple-element.93.dgate_ref, bf16[8,2,128,1024]{3,2,1,0:T(8,128)(2,1)} %bitcast.39, ...), custom_call_target="tpu_custom_call" | custom-call | flops 4000000000 | bytes 4000000 | tf_op jit(solution)/shard_map/products/pallas_call | solution.py:1041
  35.2 1.7 %collective-permute-start.3 = (bf16[256,1024]{1,0:T(8,128)(2,1)S(1)}, bf16[256,1024]{1,0:T(8,128)(2,1)S(1)}, u32[]{:S(2)}, u32[]{:S(2)}) collective-permute-start(bf16[256,1024]{1,0:T(8,128)(2,1)S(1)} %get-tuple-element.98), channel_id=1, source_target_pairs={{0,4},{2,6},{4,0},{6,2},{8,12},{10,14},{12,8},{14,10},{16,20},{18,... | collective-permute-start | bytes 1572872 | tf_op jit(solution)/shard_map/ppermute | solution.py:1152
  36.9 1.3 %collective-permute-start.4 = (bf16[256,1024]{1,0:T(8,128)(2,1)S(1)}, bf16[256,1024]{1,0:T(8,128)(2,1)S(1)}, u32[]{:S(2)}, u32[]{:S(2)}) collective-permute-start(bf16[256,1024]{1,0:T(8,128)(2,1)S(1)} %get-tuple-element.99), channel_id=1, source_target_pairs={{0,8},{2,10},{4,12},{6,14},{8,0},{10,2},{12,4},{14,6},{16,24},{18,... | collective-permute-start | bytes 1572872 | tf_op jit(solution)/shard_map/ppermute | solution.py:1152
  38.2 25.3 %scan_backward.1 = (bf16[256,128]{1,0:T(8,128)(2,1)}, f32[256,1024]{1,0:T(8,128)}, bf16[256,1024]{1,0:T(8,128)(2,1)}, f32[128,128]{1,0:T(8,128)}, f32[2,1024]{1,0:T(2,128)}) custom-call(s32[4]{0:T(128)S(1)} %pad_add_fusion.place_ref, f32[256,32]{1,0:T(8,128)} %get-tuple-element.101.bc_ref, f32[128,128]{1,0:T(8,128)} %get-tuple-element.102.decay_ref.refs_9_, ...), custom_call_target="tpu_custom_call" | custom-call | tf_op jit(solution)/shard_map/scan_backward/pallas_call | solution.py:690
  63.6 1.4 %collective-permute-start.6 = (bf16[256,128]{1,0:T(8,128)(2,1)}, bf16[256,128]{1,0:T(8,128)(2,1)S(1)}, u32[]{:S(2)}, u32[]{:S(2)}) collective-permute-start(bf16[256,128]{1,0:T(8,128)(2,1)} %get-tuple-element.111.refs_0_), channel_id=1, source_target_pairs={{0,1},{1,0},{2,3},{3,2},{4,5},{5,4},{6,7},{7,6},{8,9},{9,8},{10,11... | collective-permute-start | bytes 196616 | tf_op jit(solution)/shard_map/ppermute | solution.py:1148
  67.0 10.5 %tail.1 = (bf16[640,1024]{1,0:T(8,128)(2,1)}, bf16[640,1024]{1,0:T(8,128)(2,1)}, bf16[256,1024]{1,0:T(8,128)(2,1)}) custom-call(s32[4]{0:T(128)S(1)} %pad_add_fusion.place_ref, s32[2,1,2]{2,1,0:T(1,128)S(1)} %copy-done.3, bf16[256,128]{1,0:T(8,128)(2,1)} %get-tuple-element.111.refs_0_, bf16[256,128]{1,0:T(8,128)(2,1)S(1)} %collective-permute-done.6.refs_1_, ...), custom_call_target="tpu_custom_call" | custom-call | flops 7000000000 | bytes 7000000 | tf_op jit(solution)/shard_map/tail/pallas_call | solution.py:930
  78.0 2.0 %collective-permute-start.8 = (bf16[640,1024]{1,0:T(8,128)(2,1)}, bf16[640,1024]{1,0:T(8,128)(2,1)S(1)}, u32[]{:S(2)}, u32[]{:S(2)}) collective-permute-start(bf16[640,1024]{1,0:T(8,128)(2,1)} %get-tuple-element.128), channel_id=1, source_target_pairs={{0,2},{2,0},{4,6},{6,4},{8,10},{10,8},{12,14},{14,12},{16,18},{18,... | collective-permute-start | bytes 3932168 | tf_op jit(solution)/shard_map/ppermute | solution.py:1152
  79.9 2.7 %collective-permute-start.12 = (bf16[64,1024]{1,0:T(8,128)(2,1)S(1)}, bf16[64,1024]{1,0:T(8,128)(2,1)S(1)}, u32[]{:S(2)}, u32[]{:S(2)}) collective-permute-start(bf16[64,1024]{1,0:T(8,128)(2,1)S(1)} %slice.116), channel_id=1, source_target_pairs={{0,16},{2,18},{4,20},{6,22},{8,24},{10,26},{12,28},{14,30},{16,0},... | collective-permute-start | bytes 393224 | tf_op jit(solution)/shard_map/ppermute | solution.py:1152
  82.7 1.2 %collective-permute-start.14 = (bf16[256,1024]{1,0:T(8,128)(2,1)}, bf16[256,1024]{1,0:T(8,128)(2,1)S(1)}, u32[]{:S(2)}, u32[]{:S(2)}) collective-permute-start(bf16[256,1024]{1,0:T(8,128)(2,1)} %get-tuple-element.130.mine_ref), channel_id=1, source_target_pairs={{0,1},{1,0},{2,3},{3,2},{4,5},{5,4},{6,7},{7,6},{8,9},{9,8},{10,11... | collective-permute-start | bytes 1572872 | tf_op jit(solution)/shard_map/ppermute | solution.py:1148
  83.9 1.5 %slice_add_fusion.4 = (bf16[160,1024]{1,0:T(8,128)(2,1)S(1)}, bf16[160,1024]{1,0:T(8,128)(2,1)S(1)}, bf16[160,1024]{1,0:T(8,128)(2,1)S(1)}, bf16[160,1024]{1,0:T(8,128)(2,1)S(1)}) fusion(bf16[640,1024]{1,0:T(8,128)(2,1)S(1)} %collective-permute-done.8, bf16[640,1024]{1,0:T(8,128)(2,1)} %get-tuple-element.125), kind=kLoop, calls=%fused_computation.8 | loop fusion | flops 655360 | bytes 3932160 | tf_op jit(solution)/shard_map/add | solution.py:1172
  85.4 2.3 %collective-permute-start.11 = (bf16[160,1024]{1,0:T(8,128)(2,1)S(1)}, bf16[160,1024]{1,0:T(8,128)(2,1)S(1)}, u32[]{:S(2)}, u32[]{:S(2)}) collective-permute-start(bf16[160,1024]{1,0:T(8,128)(2,1)S(1)} %get-tuple-element.163), channel_id=1, source_target_pairs={{0,12},{2,14},{4,8},{6,10},{8,4},{10,6},{12,0},{14,2},{16,28},{18,... | collective-permute-start | bytes 983048 | tf_op jit(solution)/shard_map/ppermute | solution.py:1152
  88.1 1.2 %collective-permute-done.12 = bf16[64,1024]{1,0:T(8,128)(2,1)S(1)} collective-permute-done((bf16[64,1024]{1,0:T(8,128)(2,1)S(1)}, bf16[64,1024]{1,0:T(8,128)(2,1)S(1)}, u32[]{:S(2)}, u32[]{:S(2)}) %collective-permute-start.12) | collective-permute-done | bytes 131104 | tf_op jit(solution)/shard_map/ppermute | solution.py:1152
  89.4 3.8 %collective-permute-start.13 = (bf16[64,1024]{1,0:T(8,128)(2,1)S(1)}, bf16[64,1024]{1,0:T(8,128)(2,1)S(1)}, u32[]{:S(2)}, u32[]{:S(2)}) collective-permute-start(bf16[64,1024]{1,0:T(8,128)(2,1)S(1)} %slice_add_fusion.8), channel_id=1, source_target_pairs={{0,0},{1,2},{2,1},{3,3},{4,4},{5,6},{6,5},{7,7},{8,8},{9,10},{10,9... | collective-permute-start | bytes 393224 | tf_op jit(solution)/shard_map/ppermute | solution.py:1161
  94.2 1.9 %collective-permute-done.14.theirs_ref = bf16[256,1024]{1,0:T(8,128)(2,1)S(1)} collective-permute-done((bf16[256,1024]{1,0:T(8,128)(2,1)}, bf16[256,1024]{1,0:T(8,128)(2,1)S(1)}, u32[]{:S(2)}, u32[]{:S(2)}) %collective-permute-start.14) | collective-permute-done | bytes 524320 | tf_op jit(solution)/shard_map/ppermute | solution.py:1148
  96.1 3.9 %finish.1 = f32[256,1024]{1,0:T(8,128)} custom-call(bf16[256,1024]{1,0:T(8,128)(2,1)} %bitcast.24, bf16[256,1024]{1,0:T(8,128)(2,1)} %get-tuple-element.130.mine_ref, bf16[256,1024]{1,0:T(8,128)(2,1)S(1)} %collective-permute-done.14.theirs_ref, bf16[256,1024]{1,0:T(8,128)(2,1)} %bitcast.27, f32[1,1024]{1,0:T(1,128)} %bitcast.34), custom_call_target="tpu_custom_call" | custom-call | tf_op jit(solution)/shard_map/finish/pallas_call | solution.py:1075
  100.1 2.9 %collective-permute-done.10 = bf16[160,1024]{1,0:T(8,128)(2,1)S(1)} collective-permute-done((bf16[160,1024]{1,0:T(8,128)(2,1)S(1)}, bf16[160,1024]{1,0:T(8,128)(2,1)S(1)}, u32[]{:S(2)}, u32[]{:S(2)}) %collective-permute-start.10) | collective-permute-done | bytes 327712 | tf_op jit(solution)/shard_map/ppermute | solution.py:1152
  103.0 1.4 %collective-permute-done.9 = bf16[160,1024]{1,0:T(8,128)(2,1)S(1)} collective-permute-done((bf16[160,1024]{1,0:T(8,128)(2,1)S(1)}, bf16[160,1024]{1,0:T(8,128)(2,1)S(1)}, u32[]{:S(2)}, u32[]{:S(2)}) %collective-permute-start.9) | collective-permute-done | bytes 327712 | tf_op jit(solution)/shard_map/ppermute | solution.py:1152
  105.3 2.7 %collective-permute-start.16 = (bf16[16,1024]{1,0:T(8,128)(2,1)S(1)}, bf16[16,1024]{1,0:T(8,128)(2,1)S(1)}, u32[]{:S(2)}, u32[]{:S(2)}) collective-permute-start(bf16[16,1024]{1,0:T(8,128)(2,1)S(1)} %get-tuple-element.140), channel_id=1, source_target_pairs={{0,16},{1,18},{2,17},{3,19},{4,20},{5,22},{6,21},{7,23},{8,24},{9,... | collective-permute-start | bytes 98312 | tf_op jit(solution)/shard_map/ppermute | solution.py:1161
  107.9 2.5 %collective-permute-start.17 = (bf16[16,1024]{1,0:T(8,128)(2,1)S(1)}, bf16[16,1024]{1,0:T(8,128)(2,1)S(1)}, u32[]{:S(2)}, u32[]{:S(2)}) collective-permute-start(bf16[16,1024]{1,0:T(8,128)(2,1)S(1)} %get-tuple-element.141), channel_id=1, source_target_pairs={{0,0},{1,2},{2,1},{3,3},{4,4},{5,6},{6,5},{7,7},{8,8},{9,10},{10,9... | collective-permute-start | bytes 98312 | tf_op jit(solution)/shard_map/ppermute | solution.py:1161
  111.2 7.8 %collective-permute-done.16.far_ref = bf16[16,1024]{1,0:T(8,128)(2,1)S(1)} collective-permute-done((bf16[16,1024]{1,0:T(8,128)(2,1)S(1)}, bf16[16,1024]{1,0:T(8,128)(2,1)S(1)}, u32[]{:S(2)}, u32[]{:S(2)}) %collective-permute-start.16) | collective-permute-done | bytes 32800 | tf_op jit(solution)/shard_map/ppermute | solution.py:1161
  119.6 1.7 %unpack.1 = (f32[64,64]{1,0:T(8,128)}, f32[64,64]{1,0:T(8,128)}, f32[2,8,128]{2,1,0:T(8,128)}, f32[8,128]{1,0:T(8,128)}, f32[4,64]{1,0:T(4,128)}, /*index=5*/f32...) custom-call(bf16[16,1024]{1,0:T(8,128)(2,1)} %copy-done.9, bf16[16,1024]{1,0:T(8,128)(2,1)} %copy-done.8, ...), custom_call_target="tpu_custom_call" | custom-call | tf_op jit(solution)/shard_map/unpack/pallas_call | solution.py:1135
  (59 shorter events, 9.1 us)
Async XLA Ops:
  0.6 11.3 %collective-permute-start.1 = (f32[8,2048]{1,0:T(8,128)}, f32[8,2048]{1,0:T(8,128)S(1)}, u32[]{:S(2)}, u32[]{:S(2)}) collective-permute-start(f32[8,2048]{1,0:T(8,128)} %alog_own_ref.1), channel_id=1, source_target_pairs={{0,1},{1,0},{2,3},{3,2},{4,5},{5,4},{6,7},{7,6},{8,9},{9,8},{10,11... | collective-permute-start | bytes 196616 | tf_op jit(solution)/shard_map/ppermute | solution.py:1148
  2.8 9.2 %collective-permute-start = (bf16[2,8,2048]{2,1,0:T(8,128)(2,1)}, bf16[2,8,2048]{2,1,0:T(8,128)(2,1)S(1)}, u32[]{:S(2)}, u32[]{:S(2)}) collective-permute-start(bf16[2,8,2048]{2,1,0:T(8,128)(2,1)} %refs_7_.1), channel_id=1, source_target_pairs={{0,1},{1,0},{2,3},{3,2},{4,5},{5,4},{6,7},{7,6},{8,9},{9,8},{10,11... | collective-permute-start | bytes 196616 | tf_op jit(solution)/shard_map/ppermute | solution.py:1148
  2.9 9.1 %copy-start.3 = (s32[2,1,2]{2,1,0:T(1,128)S(1)}, s32[2,1,2]{2,1,0:T(1,128)}, u32[]{:S(2)}) copy-start(s32[2,1,2]{2,1,0:T(1,128)} %len_ref.5) | copy-start | bytes 52
  12.0 16.1 %copy-start.2 = (bf16[2,8,2048]{2,1,0:T(8,128)(2,1)}, bf16[2,8,2048]{2,1,0:T(8,128)(2,1)S(1)}, u32[]{:S(2)}) copy-start(bf16[2,8,2048]{2,1,0:T(8,128)(2,1)S(1)} %collective-permute-done.bc_other_ref.refs_8_) | copy-start | bytes 196612
  28.1 6.9 %collective-permute-start.2 = (bf16[1024,1024]{1,0:T(8,128)(2,1)}, bf16[1024,1024]{1,0:T(8,128)(2,1)S(1)}, u32[]{:S(2)}, u32[]{:S(2)}) collective-permute-start(bf16[1024,1024]{1,0:T(8,128)(2,1)} %get-tuple-element.91), channel_id=1, source_target_pairs={{0,2},{2,0},{4,6},{6,4},{8,10},{10,8},{12,14},{14,12},{16,18},{18,... | collective-permute-start | bytes 6291464 | tf_op jit(solution)/shard_map/ppermute | solution.py:1152
  35.2 28.4 %collective-permute-start.3 = (bf16[256,1024]{1,0:T(8,128)(2,1)S(1)}, bf16[256,1024]{1,0:T(8,128)(2,1)S(1)}, u32[]{:S(2)}, u32[]{:S(2)}) collective-permute-start(bf16[256,1024]{1,0:T(8,128)(2,1)S(1)} %get-tuple-element.98), channel_id=1, source_target_pairs={{0,4},{2,6},{4,0},{6,2},{8,12},{10,14},{12,8},{14,10},{16,20},{18,... | collective-permute-start | bytes 1572872 | tf_op jit(solution)/shard_map/ppermute | solution.py:1152
  36.9 26.7 %collective-permute-start.4 = (bf16[256,1024]{1,0:T(8,128)(2,1)S(1)}, bf16[256,1024]{1,0:T(8,128)(2,1)S(1)}, u32[]{:S(2)}, u32[]{:S(2)}) collective-permute-start(bf16[256,1024]{1,0:T(8,128)(2,1)S(1)} %get-tuple-element.99), channel_id=1, source_target_pairs={{0,8},{2,10},{4,12},{6,14},{8,0},{10,2},{12,4},{14,6},{16,24},{18,... | collective-permute-start | bytes 1572872 | tf_op jit(solution)/shard_map/ppermute | solution.py:1152
  38.2 25.4 %collective-permute-start.5 = (bf16[256,1024]{1,0:T(8,128)(2,1)S(1)}, bf16[256,1024]{1,0:T(8,128)(2,1)S(1)}, u32[]{:S(2)}, u32[]{:S(2)}) collective-permute-start(bf16[256,1024]{1,0:T(8,128)(2,1)S(1)} %get-tuple-element.100), channel_id=1, source_target_pairs={{0,12},{2,14},{4,8},{6,10},{8,4},{10,6},{12,0},{14,2},{16,28},{18,... | collective-permute-start | bytes 1572872 | tf_op jit(solution)/shard_map/ppermute | solution.py:1152
  63.6 3.4 %collective-permute-start.6 = (bf16[256,128]{1,0:T(8,128)(2,1)}, bf16[256,128]{1,0:T(8,128)(2,1)S(1)}, u32[]{:S(2)}, u32[]{:S(2)}) collective-permute-start(bf16[256,128]{1,0:T(8,128)(2,1)} %get-tuple-element.111.refs_0_), channel_id=1, source_target_pairs={{0,1},{1,0},{2,3},{3,2},{4,5},{5,4},{6,7},{7,6},{8,9},{9,8},{10,11... | collective-permute-start | bytes 196616 | tf_op jit(solution)/shard_map/ppermute | solution.py:1148
  65.4 12.5 %collective-permute-start.7 = (bf16[256,1024]{1,0:T(8,128)(2,1)S(1)}, bf16[256,1024]{1,0:T(8,128)(2,1)S(1)}, u32[]{:S(2)}, u32[]{:S(2)}) collective-permute-start(bf16[256,1024]{1,0:T(8,128)(2,1)S(1)} %copy-done.6), channel_id=1, source_target_pairs={{0,1},{1,0},{2,3},{3,2},{4,5},{5,4},{6,7},{7,6},{8,9},{9,8},{10,11... | collective-permute-start | bytes 1572872 | tf_op jit(solution)/shard_map/ppermute | solution.py:1148
  78.0 6.0 %collective-permute-start.8 = (bf16[640,1024]{1,0:T(8,128)(2,1)}, bf16[640,1024]{1,0:T(8,128)(2,1)S(1)}, u32[]{:S(2)}, u32[]{:S(2)}) collective-permute-start(bf16[640,1024]{1,0:T(8,128)(2,1)} %get-tuple-element.128), channel_id=1, source_target_pairs={{0,2},{2,0},{4,6},{6,4},{8,10},{10,8},{12,14},{14,12},{16,18},{18,... | collective-permute-start | bytes 3932168 | tf_op jit(solution)/shard_map/ppermute | solution.py:1152
  79.9 9.4 %collective-permute-start.12 = (bf16[64,1024]{1,0:T(8,128)(2,1)S(1)}, bf16[64,1024]{1,0:T(8,128)(2,1)S(1)}, u32[]{:S(2)}, u32[]{:S(2)}) collective-permute-start(bf16[64,1024]{1,0:T(8,128)(2,1)S(1)} %slice.116), channel_id=1, source_target_pairs={{0,16},{2,18},{4,20},{6,22},{8,24},{10,26},{12,28},{14,30},{16,0},... | collective-permute-start | bytes 393224 | tf_op jit(solution)/shard_map/ppermute | solution.py:1152
  82.7 13.4 %collective-permute-start.14 = (bf16[256,1024]{1,0:T(8,128)(2,1)}, bf16[256,1024]{1,0:T(8,128)(2,1)S(1)}, u32[]{:S(2)}, u32[]{:S(2)}) collective-permute-start(bf16[256,1024]{1,0:T(8,128)(2,1)} %get-tuple-element.130.mine_ref), channel_id=1, source_target_pairs={{0,1},{1,0},{2,3},{3,2},{4,5},{5,4},{6,7},{7,6},{8,9},{9,8},{10,11... | collective-permute-start | bytes 1572872 | tf_op jit(solution)/shard_map/ppermute | solution.py:1148
  83.9 9.2 %copy-start.5 = (bf16[2,128,1024]{2,1,0:T(8,128)(2,1)S(1)}, bf16[2,128,1024]{2,1,0:T(8,128)(2,1)}, u32[]{:S(2)}) copy-start(bf16[2,128,1024]{2,1,0:T(8,128)(2,1)} %param.14) | copy-start | bytes 1572868
  85.4 14.7 %collective-permute-start.11 = (bf16[160,1024]{1,0:T(8,128)(2,1)S(1)}, bf16[160,1024]{1,0:T(8,128)(2,1)S(1)}, u32[]{:S(2)}, u32[]{:S(2)}) collective-permute-start(bf16[160,1024]{1,0:T(8,128)(2,1)S(1)} %get-tuple-element.163), channel_id=1, source_target_pairs={{0,12},{2,14},{4,8},{6,10},{8,4},{10,6},{12,0},{14,2},{16,28},{18,... | collective-permute-start | bytes 983048 | tf_op jit(solution)/shard_map/ppermute | solution.py:1152
  87.7 15.3 %collective-permute-start.10 = (bf16[160,1024]{1,0:T(8,128)(2,1)S(1)}, bf16[160,1024]{1,0:T(8,128)(2,1)S(1)}, u32[]{:S(2)}, u32[]{:S(2)}) collective-permute-start(bf16[160,1024]{1,0:T(8,128)(2,1)S(1)} %get-tuple-element.164), channel_id=1, source_target_pairs={{0,8},{2,10},{4,12},{6,14},{8,0},{10,2},{12,4},{14,6},{16,24},{18,... | collective-permute-start | bytes 983048 | tf_op jit(solution)/shard_map/ppermute | solution.py:1152
  87.8 16.5 %collective-permute-start.9 = (bf16[160,1024]{1,0:T(8,128)(2,1)S(1)}, bf16[160,1024]{1,0:T(8,128)(2,1)S(1)}, u32[]{:S(2)}, u32[]{:S(2)}) collective-permute-start(bf16[160,1024]{1,0:T(8,128)(2,1)S(1)} %get-tuple-element.165), channel_id=1, source_target_pairs={{0,4},{2,6},{4,0},{6,2},{8,12},{10,14},{12,8},{14,10},{16,20},{18,... | collective-permute-start | bytes 983048 | tf_op jit(solution)/shard_map/ppermute | solution.py:1152
  89.4 10.7 %collective-permute-start.13 = (bf16[64,1024]{1,0:T(8,128)(2,1)S(1)}, bf16[64,1024]{1,0:T(8,128)(2,1)S(1)}, u32[]{:S(2)}, u32[]{:S(2)}) collective-permute-start(bf16[64,1024]{1,0:T(8,128)(2,1)S(1)} %slice_add_fusion.8), channel_id=1, source_target_pairs={{0,0},{1,2},{2,1},{3,3},{4,4},{5,6},{6,5},{7,7},{8,8},{9,10},{10,9... | collective-permute-start | bytes 393224 | tf_op jit(solution)/shard_map/ppermute | solution.py:1161
  100.1 19.0 %copy-start.7 = (bf16[64,1024]{1,0:T(8,128)(2,1)}, bf16[64,1024]{1,0:T(8,128)(2,1)S(1)}, u32[]{:S(2)}) copy-start(bf16[64,1024]{1,0:T(8,128)(2,1)S(1)} %collective-permute-done.13.out_ref) | copy-start | bytes 393220
  104.6 14.3 %collective-permute-start.15 = (bf16[64,1024]{1,0:T(8,128)(2,1)S(1)}, bf16[64,1024]{1,0:T(8,128)(2,1)S(1)}, u32[]{:S(2)}, u32[]{:S(2)}) collective-permute-start(bf16[64,1024]{1,0:T(8,128)(2,1)S(1)} %get-tuple-element.139), channel_id=1, source_target_pairs={{0,16},{2,18},{4,20},{6,22},{8,24},{10,26},{12,28},{14,30},{16,0},... | collective-permute-start | bytes 393224 | tf_op jit(solution)/shard_map/ppermute | solution.py:1152
  105.3 13.7 %collective-permute-start.16 = (bf16[16,1024]{1,0:T(8,128)(2,1)S(1)}, bf16[16,1024]{1,0:T(8,128)(2,1)S(1)}, u32[]{:S(2)}, u32[]{:S(2)}) collective-permute-start(bf16[16,1024]{1,0:T(8,128)(2,1)S(1)} %get-tuple-element.140), channel_id=1, source_target_pairs={{0,16},{1,18},{2,17},{3,19},{4,20},{5,22},{6,21},{7,23},{8,24},{9,... | collective-permute-start | bytes 98312 | tf_op jit(solution)/shard_map/ppermute | solution.py:1161
  107.9 11.1 %collective-permute-start.17 = (bf16[16,1024]{1,0:T(8,128)(2,1)S(1)}, bf16[16,1024]{1,0:T(8,128)(2,1)S(1)}, u32[]{:S(2)}, u32[]{:S(2)}) collective-permute-start(bf16[16,1024]{1,0:T(8,128)(2,1)S(1)} %get-tuple-element.141), channel_id=1, source_target_pairs={{0,0},{1,2},{2,1},{3,3},{4,4},{5,6},{6,5},{7,7},{8,8},{9,10},{10,9... | collective-permute-start | bytes 98312 | tf_op jit(solution)/shard_map/ppermute | solution.py:1161
  110.4 10.8 %collective-permute-start.19 = (bf16[64,1024]{1,0:T(8,128)(2,1)S(1)}, bf16[64,1024]{1,0:T(8,128)(2,1)S(1)}, u32[]{:S(2)}, u32[]{:S(2)}) collective-permute-start(bf16[64,1024]{1,0:T(8,128)(2,1)S(1)} %get-tuple-element.169), channel_id=1, source_target_pairs={{0,16},{2,18},{4,20},{6,22},{8,24},{10,26},{12,28},{14,30},{16,0},... | collective-permute-start | bytes 393224 | tf_op jit(solution)/shard_map/ppermute | solution.py:1152
  119.0 3.2 %collective-permute-start.18 = (bf16[16,128]{1,0:T(8,128)(2,1)S(1)}, bf16[16,128]{1,0:T(8,128)(2,1)S(1)}, u32[]{:S(2)}, u32[]{:S(2)}) collective-permute-start(bf16[16,128]{1,0:T(8,128)(2,1)S(1)} %add_convert_fusion.3), channel_id=1, source_target_pairs={{0,2},{2,0},{4,6},{6,4},{8,10},{10,8},{12,14},{14,12},{16,18},{18,... | collective-permute-start | bytes 12296 | tf_op jit(solution)/shard_map/ppermute | solution.py:1152
  (6 other events, 27.1 us)
